TPU v7x, 32 devices: a whole 2x2x4 slice. The times are simulated.
32 devices in a mesh: row: 4 (over y, x), col: 8 (over z, core).
Axes of the slice: x: 2, y: 2, z: 4, core: 2. Of those that a mesh axis runs over, the one named last changes fastest.
Arguments:
- rhs: float32 [32, 16384], P('row', 'col'), may hold values from -60 to 60
- flex_tiles: float32 [32768, 1024], P('row', 'col'), may hold values from -0.25 to 0.25
- flex_cols: int32 [64, 32], P('row', 'col'), may hold values from 0 to 15, as said below
- stiff_tiles: float32 [32768, 1024], P('row', 'col'), may hold values from -0.25 to 0.25
- stiff_cols: int32 [64, 32], P('row', 'col'), may hold values from 0 to 15, as said below
- deflation: float32 [128, 16384], P('row', 'col'), may hold values from -0.375 to 0.375
- coarse_rows: float32 [1024, 1024], P(('row', 'col')), may hold values from -5 to 5, as said below
- face_rows: int32 [16, 1024], P('row', 'col'), may hold values from 0 to 2047, as said below
- face_len: int32 [4, 32], P('row', 'col'), may hold values from 0 to 128, as said below
Outputs:
- solution: float32 [32, 16384], P('row', 'col')
- residual: float32 [32, 16384], P('row', 'col')
- correction: float32 [32, 16384], P('row', 'col')
Inputs may be any that keep to these rules, and one draw needn't show every extreme that they name: `flex_cols`: row b of a subdomain's block list names 4 different block columns, the first being b. `stiff_cols`: row b of a subdomain's block list names 4 different block columns, the first being b. `coarse_rows`: the whole matrix is symmetric. `face_rows`: the four lists of a subdomain name 512 different multipliers of it. `face_len`: the two subdomains of a face give it the same length; faces on the grid's boundary have length 0, inner faces at least 32.
All inputs are finite; a program needn't handle non-finite values.
Results may differ from a plain program's by a relative error of at most 0.0003.
Values sent between devices are 32-bit elements; how exact they have to be, the bound alone decides.
No kernel may reach another device: no remote copies, remote signals or barrier semaphores. Data moves between devices by JAX's collectives and lax.ppermute only.
A program may use at most 64 MiB of HBM per device.

v0:
```python
import functools
from types import SimpleNamespace

import jax
import jax.numpy as jnp
from jax import lax
from jax.experimental import pallas as pl
from jax.experimental.pallas import tpu as pltpu
from jax.sharding import PartitionSpec as P

ITERS = 3
START, FIRST, MIDDLE, LAST = range(4)
LANE = 128
AXES = ("row", "col")
F32, BF16, I32 = jnp.float32, jnp.bfloat16, jnp.int32
NT = (((1,), (1,)), ((), ()))

SMEM = pl.BlockSpec(memory_space=pltpu.SMEM)
VMEM = pl.BlockSpec(memory_space=pltpu.VMEM)
HBM = pl.BlockSpec(memory_space=pltpu.HBM)


def held(shape, dtype=F32):
    return pltpu.VMEM(shape, dtype)


def in_hbm(*arrays):
    return [pltpu.with_memory_space_constraint(x, pltpu.HBM) for x in arrays]


def call(body, outs, specs, name, scratch=(), out_specs=None):
    return pl.pallas_call(
        body,
        out_shape=outs,
        in_specs=specs,
        out_specs=out_specs or jax.tree.map(lambda _: VMEM, outs),
        scratch_shapes=list(scratch),
        compiler_params=pltpu.CompilerParams(vmem_limit_bytes=32 * 1024 * 1024),
        name=name,
    )


def split(x):
    hi = x.astype(BF16)
    return hi, (x - hi.astype(F32)).astype(BF16)


def stacked(x):
    return jnp.concatenate(split(x), axis=0)


def iota(shape, dim):
    return lax.broadcasted_iota(I32, shape, dim)


def pick_lanes(tiles, index):
    rows = tiles[0].shape[0]
    index = jnp.broadcast_to(index, (rows, LANE))
    block, lane = index // LANE, index % LANE
    out = jnp.zeros((rows, LANE), F32)
    for b, tile in enumerate(tiles):
        out = jnp.where(block == b, jnp.take_along_axis(tile, lane, axis=1), out)
    return out


def tiles_of(x):
    return [x[:, b * LANE : (b + 1) * LANE] for b in range(x.shape[1] // LANE)]


def neighbours(pos, count_rows, count_cols):
    i, j = pos[0], pos[1]
    out = []
    for at, count, low in ((i, count_rows, 0), (j, count_cols, 2)):
        even = at % 2 == 0
        for up in (even, jnp.logical_not(even)):
            other = jnp.where(up, at + 1, at - 1)
            there = jnp.logical_and(other >= 0, other < count)
            other = jnp.clip(other, 0, count - 1)
            device = other * count_cols + j if low == 0 else i * count_cols + other
            out.append((jnp.where(up, low + 1, low), device, there))
    return out


def pack(coefs, dots, place):
    rows, width = coefs.shape[0], LANE // 4
    load, lane = iota((rows, LANE), 0), iota((rows, LANE), 1)
    kept = jnp.where(lane // width == (load + place) % 4, coefs, 0.0)
    low = jnp.sum(jnp.where(load < 4, kept, 0.0), axis=0, keepdims=True)
    high = jnp.sum(jnp.where(load >= 4, kept, 0.0), axis=0, keepdims=True)
    scalars = jnp.zeros((rows, LANE), F32)
    for k, dot in enumerate(dots):
        scalars = jnp.where(lane == load * 16 + k, dot, scalars)
    scalars = jnp.sum(scalars, axis=0, keepdims=True)
    return jnp.concatenate([low, high, scalars, jnp.zeros_like(scalars)], axis=0)


def unpack(slot, count, loads):
    width = LANE // 4
    load, lane = iota((loads, LANE), 0), iota((loads, LANE), 1)
    source = (lane // width - load) % 4
    total = jnp.zeros((4, LANE), F32)
    out = []
    for g in range(count // 4):
        mixed = jnp.zeros((loads, LANE), F32)
        for j in range(4):
            piece = slot(4 * g + j)
            total = total + piece
            mixed = jnp.where(source == j, jnp.where(load < 4, piece[0:1], piece[1:2]), mixed)
        lined = mixed
        for q in range(1, 4):
            lined = jnp.where(load % 4 == q, pltpu.roll(mixed, LANE - q * width, axis=1), lined)
        out.append(lined)
    row = jnp.broadcast_to(total[2:3], (loads, LANE))
    dots = [
        jnp.sum(jnp.where(lane == load * 16 + k, row, 0.0), axis=1, keepdims=True) for k in range(4)
    ]
    return jnp.concatenate(out, axis=1), dots


def coefficients(field, basis):
    out = lax.dot_general(stacked(field), basis[...], NT, preferred_element_type=F32)
    out = out[: field.shape[0]] + out[field.shape[0] :]
    return out + pltpu.roll(out, LANE // 4, axis=1)


def write_slots(slots, packed, traces, sides):
    slots[...] = jnp.zeros_like(slots)
    slots[:, slots.shape[1] - 1] = jnp.broadcast_to(packed[None], (slots.shape[0],) + packed.shape)
    for trace, (_, device, there) in zip(traces, sides):

        @pl.when(there)
        def _():
            slots[device, 0] = trace[0:4]
            slots[device, 1] = trace[4:8]


def lead_kernel(grid, pos, *refs):
    sources, (slots, basis, faces), targets, (lengths, rows, sems) = refs[:5], refs[5:8], refs[8:11], refs[11:]
    copies = []
    for k, (src, dst) in enumerate(zip(sources, targets + (rows, lengths))):
        copies.append(pltpu.make_async_copy(src, dst, sems.at[k]))
        copies[-1].start()
    rhs, deflation, _ = targets
    for copy in copies:
        copy.wait()
    sides = neighbours(pos, *grid)
    hi, lo = split(deflation[...])
    basis[...] = jnp.concatenate([hi, lo, hi, lo], axis=0)
    field = rhs[...]
    coefs = coefficients(field, basis)
    tiles = tiles_of(field)
    traces = []
    lane = iota((1, LANE), 1)
    for g, (face, _, _) in enumerate(sides):
        index = rows[pl.ds(face, 1), :]
        here = iota(lengths.shape, 1) == face
        live = jnp.sum(jnp.where(here, lengths[...], 0), axis=1, keepdims=True)
        faces[g : g + 1, :] = index
        faces[g + 4 : g + 5, :] = jnp.where(lane < live, 1, 0)
        traces.append(pick_lanes(tiles, index))
    packed = pack(coefs, (), (pos[0] * grid[1] + pos[1]) % 4)
    write_slots(slots, packed, traces, sides)


def copies_kernel(deflation, coarse, faces, *outs):
    wide = coarse.shape[1]
    tiles = tiles_of(deflation[...])
    for g, out in enumerate(outs):
        out[:, :wide] = coarse[...]
        out[:, wide:] = pick_lanes(tiles, faces[g : g + 1, :])


def prepare_kernel(coarse, faces, *refs):
    received, (weights, partner_basis, inverse) = refs[:4], refs[4:]
    wide = coarse.shape[1]
    defl = coarse.shape[0]
    weights_own = split(coarse[...])
    partner_basis[...] = jnp.zeros_like(partner_basis)
    for g, ref in enumerate(received):
        for half, part in enumerate(split(ref[:, :wide])):
            weights[half * 256 + g * defl : half * 256 + (g + 1) * defl, :] = part
        for half, part in enumerate(weights_own):
            at = half * 256 + LANE + g * defl
            weights[at : at + defl, :] = part
        for half, part in enumerate(split(ref[:, wide:])):
            at = half * LANE + g * defl
            partner_basis[at : at + defl, g * LANE : (g + 1) * LANE] = part
    columns = [
        jnp.transpose(jnp.broadcast_to(faces[g : g + 1, :].astype(F32), (LANE, LANE)))
        for g in range(4)
    ]
    slot, lane = iota((LANE, LANE), 0), iota((LANE, LANE), 1)
    for b in range(inverse.shape[0]):
        found = jnp.zeros((LANE, LANE), F32)
        here = (lane + b * LANE).astype(F32)
        for g in range(4):
            found = jnp.where(columns[g] == here, (slot + (g * LANE + 1)).astype(F32), found)
        inverse[b : b + 1, :] = jnp.sum(found, axis=0, keepdims=True).astype(I32) - 1


def forward(cols, tiles, src, dst, rows):
    per_row, blocks = cols.shape
    deep = per_row * LANE
    for b in range(blocks):
        lhs = jnp.concatenate([src[cols[k, b]] for k in range(per_row)], axis=1)
        out = jnp.dot(lhs, tiles(b), preferred_element_type=F32)
        out = out[:, :LANE] + out[:, LANE:]
        dst[b] = jnp.concatenate([stacked(out[at : at + n] + out[at + n : at + 2 * n]) for at, n in rows], axis=0)


def backward(cols, tiles, src, total, rows):
    per_row, blocks = cols.shape
    total[...] = jnp.zeros_like(total)
    for b in range(blocks):
        lhs = jnp.concatenate([src[b], src[b]], axis=1)
        out = lax.dot_general(lhs, tiles(b), NT, preferred_element_type=F32)
        out = jnp.concatenate([out[at : at + n] + out[at + n : at + 2 * n] for at, n in rows], axis=0)
        for k in range(per_row):
            total[cols[k, b]] += out[:, k * LANE : (k + 1) * LANE]


def restack(total, dst, rows):
    for b in range(dst.shape[0]):
        whole, parts, at = total[b], [], 0
        for _, n in rows:
            parts.append(stacked(whole[at : at + n]))
            at += n
        dst[b] = jnp.concatenate(parts, axis=0)


PARTS = 4


def block_of(tiles, per_row):
    deep = per_row * LANE
    return lambda b: tiles[b * deep : (b + 1) * deep, :]


def transfer(source, target, sems, parts=1):
    step = source.shape[0] // parts
    copies = []
    for k in range(parts):
        at = pl.ds(k * step, step)
        copies.append(pltpu.make_async_copy(source.at[at], target.at[at], sems.at[k]))
        copies[-1].start()
    return copies


def wait(copies):
    for copy in copies:
        copy.wait()


def first_local_kernel(
    flex_raw, stiff_raw, rhs, deflation, flex_list, stiff_list,
    flex_out, stiff_out, local, local_basis,
    first, second, total, raw_first, raw_second, flex, stiff, flex_cols, stiff_cols, sems,
):
    per_row, blocks = flex_cols.shape
    deep = per_row * LANE
    arriving = (
        transfer(flex_raw, raw_first, sems.at[0], PARTS),
        transfer(stiff_raw, raw_second, sems.at[1], PARTS),
    )
    lists = transfer(flex_list, flex_cols, sems.at[2]) + transfer(stiff_list, stiff_cols, sems.at[3])
    loads, defl = rhs.shape[0], deflation.shape[0]
    rows = ((0, loads), (2 * loads, defl))
    for b in range(blocks):
        at = slice(b * LANE, (b + 1) * LANE)
        first[b] = jnp.concatenate([stacked(rhs[:, at]), stacked(deflation[:, at])], axis=0)

    def convert(raw, out, b):
        hi, lo = split(raw[b * deep : (b + 1) * deep, :])
        out[b * deep : (b + 1) * deep, :LANE] = hi
        out[b * deep : (b + 1) * deep, LANE:] = lo

    def converted(raw, out):
        def tiles(b):
            convert(raw, out, b)
            return block_of(out, per_row)(b)

        return tiles

    wait(lists)
    for copy in arriving[0]:
        copy.wait()
    forward(flex_cols, converted(raw_first, flex), first, second, rows)
    leaving = transfer(flex, flex_out, sems.at[2], PARTS)
    for copy in arriving[1]:
        copy.wait()
    forward(stiff_cols, converted(raw_second, stiff), second, first, rows)
    leaving += transfer(stiff, stiff_out, sems.at[3], PARTS)
    backward(stiff_cols, block_of(stiff, per_row), first, total, rows)
    restack(total, second, rows)
    backward(flex_cols, block_of(flex, per_row), second, total, rows)
    for b in range(blocks):
        at = slice(b * LANE, (b + 1) * LANE)
        local[:, at] = total[b][:loads]
        hi, lo = split(total[b][loads:])
        local_basis[:, at] = jnp.concatenate([hi, lo, hi, lo], axis=0)
    wait(leaving)


def local_kernel(
    flex_held, stiff_held, field, flex_list, stiff_list,
    local, first, second, total, flex, stiff, flex_cols, stiff_cols, sems,
):
    per_row, blocks = flex_cols.shape
    lists = transfer(flex_list, flex_cols, sems.at[2]) + transfer(stiff_list, stiff_cols, sems.at[3])
    arriving = (
        transfer(flex_held, flex, sems.at[0], PARTS),
        transfer(stiff_held, stiff, sems.at[1], PARTS),
    )
    rows = ((0, field.shape[0]),)
    for b in range(blocks):
        first[b] = stacked(field[:, b * LANE : (b + 1) * LANE])
    wait(lists)
    wait(arriving[0])
    forward(flex_cols, block_of(flex, per_row), first, second, rows)
    wait(arriving[1])
    forward(stiff_cols, block_of(stiff, per_row), second, first, rows)
    backward(stiff_cols, block_of(stiff, per_row), first, total, rows)
    restack(total, second, rows)
    backward(flex_cols, block_of(flex, per_row), second, total, rows)
    for b in range(blocks):
        local[:, b * LANE : (b + 1) * LANE] = total[b]


def step_kernel(grid, kind, names, out_names, *refs):
    old = SimpleNamespace(**dict(zip(names, refs)))
    out = SimpleNamespace(**dict(zip(out_names, refs[len(names) :])))
    pos, received = old.pos, old.received
    loads = old.residual.shape[0]
    count = received.shape[0]
    last = received.shape[1] - 1
    sides = neighbours(pos, *grid)

    coefs, dots = unpack(lambda s: received[s, last], count, loads)
    both = lax.dot_general(stacked(coefs), old.weights[...], NT, preferred_element_type=F32)
    both = both[:loads] + both[loads:]
    energy = both[:, :256] + both[:, 256:]

    def partner_traces():
        traces = []
        for _, device, there in sides:
            trace = jnp.concatenate([received[device, 0], received[device, 1]], axis=0)
            traces.append(jnp.where(there, trace, 0.0))
        return jnp.concatenate(traces, axis=1)

    keep = {}
    if kind == START:
        residual, local_residual = old.residual[...], old.local_after[...]
        energy_residual, partner_residual = energy, partner_traces()
    else:
        if kind == FIRST:
            curvature, descent = dots[0], dots[1]
            direction, image, energy_image = old.correction[...], old.after[...], energy
            local_image, partner_image = old.local_after[...], partner_traces()
        else:
            energy_sum, project_sum, cross_sum, old_sum = dots
            before = jnp.max(old.curvature[...], axis=1, keepdims=True)
            blend = -cross_sum / before
            curvature = energy_sum + 2.0 * blend * cross_sum + blend * blend * before
            descent = project_sum + blend * old_sum
            direction = old.correction[...] + blend * old.direction[...]
            image = old.after[...] + blend * old.image[...]
            energy_image = energy + blend * old.energy_image[...]
            if kind == MIDDLE:
                local_image = old.local_after[...] + blend * old.local_image[...]
                partner_image = partner_traces() + blend * old.partner_image[...]
        step = descent / curvature
        residual = old.residual[...] - step * image
        energy_residual = old.energy_residual[...] - step * energy_image
        out.solution[...] = step * direction + (0.0 if kind == FIRST else old.solution[...])
        keep.update(residual=residual, direction=direction, image=image, energy_image=energy_image)
        keep.update(curvature=jnp.broadcast_to(curvature, (loads, LANE)))
        if kind != LAST:
            local_residual = old.local_residual[...] - step * local_image
            partner_residual = old.partner_residual[...] - step * partner_image
            keep.update(local_image=local_image, partner_image=partner_image)
    keep.update(energy_residual=energy_residual)

    own = energy_residual[:, LANE:]
    hi, lo = split(own)
    lane = iota(own.shape, 1)
    lhs = jnp.where(lane < LANE // 2, hi.astype(F32), lo.astype(F32)).astype(BF16)
    correction = residual + jnp.dot(lhs, old.basis[...], preferred_element_type=F32)
    keep.update(correction=correction)
    if kind != LAST:
        local = local_residual + jnp.dot(lhs, old.local_basis[...], preferred_element_type=F32)
        hi, lo = split(energy_residual[:, :LANE])
        pairs = jnp.concatenate(
            [jnp.concatenate([hi, hi], axis=1), jnp.concatenate([lo, lo], axis=1)], axis=0
        )
        other = jnp.dot(pairs, old.partner_basis[...], preferred_element_type=F32)
        partner = partner_residual + other[:loads] + other[loads:]
        faces, inverse = old.faces, old.inverse
        tiles = tiles_of(correction)
        jumps = []
        for g in range(4):
            trace = pick_lanes(tiles, faces[g : g + 1, :])
            jump = trace - partner[:, g * LANE : (g + 1) * LANE]
            jumps.append(jnp.where(faces[g + 4 : g + 5, :] > 0, jump, 0.0))
        pieces = []
        for b in range(len(tiles)):
            code = inverse[b : b + 1, :]
            pieces.append(pick_lanes(jumps, jnp.where(code < 0, 4 * LANE, code)))
        after = correction + local + jnp.concatenate(pieces, axis=1)

        dot = lambda a, b: jnp.sum(a * b, axis=1, keepdims=True)
        sums = [dot(correction, after), dot(residual, correction)]
        if kind != START:
            sums += [dot(correction, image), dot(residual, direction)]
        packed = pack(coefficients(after, old.basis), sums, (pos[0] * grid[1] + pos[1]) % 4)
        traces = []
        if kind != MIDDLE:
            tiles = tiles_of(after)
            traces = [pick_lanes(tiles, faces[g : g + 1, :]) for g in range(4)]
        write_slots(out.slots, packed, traces, sides)
        keep.update(after=after, partner_residual=partner_residual, local_residual=local_residual)
    for k, v in keep.items():
        if hasattr(out, k):
            getattr(out, k)[...] = v


def exchange(slots):
    return lax.all_to_all(slots, AXES, 0, 0)


def pairs_of(count, odd):
    low = [(k, k + 1) for k in range(odd, count - 1, 2)]
    return low + [(b, a) for a, b in low]


def shards(
    grid, rhs, flex_tiles, flex_cols, stiff_tiles, stiff_cols, deflation, coarse_rows, face_rows, face_len
):
    loads, wide = rhs.shape
    defl, coarse = coarse_rows.shape
    blocks, per_row = flex_cols.shape
    count = grid[0] * grid[1]
    pos = jnp.stack([lax.axis_index("row"), lax.axis_index("col")]).astype(I32)
    whole = (loads, wide)
    slots = held((count, 3, 4, LANE))

    slots_now, basis, faces, rhs, deflation, coarse_rows = call(
        functools.partial(lead_kernel, grid),
        (
            slots,
            held((4 * defl, wide), BF16),
            held((8, LANE), I32),
            held(whole),
            held(deflation.shape),
            held(coarse_rows.shape),
        ),
        [SMEM] + [HBM] * 5,
        "lead",
        scratch=(pltpu.VMEM(face_len.shape, I32), pltpu.VMEM(face_rows.shape, I32), pltpu.SemaphoreType.DMA((5,))),
    )(pos, *in_hbm(rhs, deflation, coarse_rows, face_rows, face_len))
    received = exchange(slots_now)

    copies = call(
        copies_kernel,
        (jax.ShapeDtypeStruct((defl, coarse + LANE), F32),) * 4,
        [VMEM, VMEM, VMEM],
        "copies",
    )(deflation, coarse_rows, faces)
    copies = [
        lax.ppermute(c, axis, pairs_of(n, odd))
        for c, (axis, n, odd) in zip(
            copies, (("row", grid[0], 0), ("row", grid[0], 1), ("col", grid[1], 0), ("col", grid[1], 1))
        )
    ]
    lists = in_hbm(flex_cols.T, stiff_cols.T)
    tiles_shape = (flex_tiles.shape[0], 2 * LANE)
    tile_scratch = (
        pltpu.VMEM(tiles_shape, BF16),
        pltpu.VMEM(tiles_shape, BF16),
        pltpu.SMEM((per_row, blocks), I32),
        pltpu.SMEM((per_row, blocks), I32),
        pltpu.SemaphoreType.DMA((4, PARTS)),
    )

    def block_scratch(rows):
        return (
            pltpu.VMEM((blocks, 2 * rows, LANE), BF16),
            pltpu.VMEM((blocks, 2 * rows, LANE), BF16),
            pltpu.VMEM((blocks, rows, LANE), F32),
        )

    flex, stiff, local, local_basis = call(
        first_local_kernel,
        (
            pltpu.HBM(tiles_shape, BF16),
            pltpu.HBM(tiles_shape, BF16),
            held(whole),
            held((4 * defl, wide), BF16),
        ),
        [HBM] * 2 + [VMEM] * 2 + [HBM] * 2,
        "first_local",
        scratch=block_scratch(loads + defl)
        + (pltpu.VMEM(flex_tiles.shape, F32), pltpu.VMEM(stiff_tiles.shape, F32))
        + tile_scratch,
        out_specs=(HBM, HBM, VMEM, VMEM),
    )(
        *in_hbm(flex_tiles, stiff_tiles),
        rhs,
        deflation,
        *lists,
    )
    weights, partner_basis, inverse = call(
        prepare_kernel,
        (held((512, coarse), BF16), held((2 * LANE, 4 * LANE), BF16), held((blocks, LANE), I32)),
        [VMEM] * 6,
        "prepare",
    )(coarse_rows, faces, *copies)

    def apply_local(field):
        return call(
            local_kernel, held(whole), [HBM] * 2 + [VMEM] + [HBM] * 2, "local", block_scratch(loads) + tile_scratch
        )(*in_hbm(flex, stiff), field, *lists)

    state = dict(
        pos=pos,
        received=received,
        weights=weights,
        basis=basis,
        local_basis=local_basis,
        partner_basis=partner_basis,
        faces=faces,
        inverse=inverse,
        residual=rhs,
        local_after=local,
        local_residual=local,
    )
    field, energy, traces = held(whole), held((loads, 256)), held((loads, 4 * LANE))
    result = jax.ShapeDtypeStruct(whole, F32)

    def step(kind, **outs):
        done = call(
            functools.partial(step_kernel, grid, kind, tuple(state), tuple(outs)),
            tuple(outs.values()),
            [SMEM] + [VMEM] * (len(state) - 1),
            f"step{kind}",
        )(*state.values())
        state.update(zip(outs, done))

    step(
        START, slots=slots, correction=field, after=field, energy_residual=energy, partner_residual=traces
    )
    for iteration in range(ITERS):
        state.update(received=exchange(state.pop("slots")))
        if iteration + 1 < ITERS:
            state.update(local_after=apply_local(state["after"]))
        kept = dict(
            solution=field, residual=field, correction=field, direction=field, image=field, after=field,
            energy_residual=energy, energy_image=energy, curvature=held((loads, LANE)), slots=slots,
        )
        more = dict(
            partner_residual=traces, local_residual=field, partner_image=traces, local_image=field
        )
        if iteration + 1 == ITERS:
            step(LAST, solution=result, residual=result, correction=result)
        elif iteration == 0 and ITERS > 2:
            step(FIRST, **kept, **more)
        else:
            kept.update(slots=held((count, 1, 4, LANE)))
            step(MIDDLE, **kept)
    return state["solution"], state["residual"], state["correction"]


def solution(mesh):
    grid = (mesh.shape["row"], mesh.shape["col"])
    return jax.shard_map(
        functools.partial(shards, grid),
        mesh=mesh,
        in_specs=(
            P("row", "col"),
            P("row", "col"),
            P("row", "col"),
            P("row", "col"),
            P("row", "col"),
            P("row", "col"),
            P(("row", "col"), None),
            P("row", "col"),
            P("row", "col"),
        ),
        out_specs=(P("row", "col"), P("row", "col"), P("row", "col")),
        check_vma=False,
    )
```

profile of v0, /device:TPU:0, one launch (start us, length us, event | category | flops | bytes accessed | tf_op | source)
XLA Modules:
  0.0 74.5 jit_solution(2865286249169281789)
XLA Ops:
  0.6 0.1 pad_add_fusion.pos.refs_0_
  0.7 2.7 %lead.1 = (f32[32,3,4,128]{3,2,1,0:T(4,128)}, bf16[128,2048]{1,0:T(8,128)(2,1)S(1)}, s32[8,128]{1,0:T(8,128)S(1)}, f32[8,2048]{1,0:T(8,128)S(1)}, f32[32,2048]{1,0:T(8,128)S(1)}, /*index=5*/f32[32,1024]{1,0:T(8,128)S(1)}) custom-call(s32[2]{0:T(128)S(1)} %pad_add_fusion.pos.refs_0_, f32[8,2048]{1,0:T(8,128)} %refs_0_.1, f32[32,2048]{1,0:T(8,128)} %refs_1_.1, ...), custom_call_target="tpu_custom_call" | custom-call | tf_op jit(solution)/shard_map/lead/pallas_call | solution.py:446
  3.4 7.3 %all-to-all-start = ((f32[32,3,4,128]{3,2,1,0:T(4,128)}), f32[32,3,4,128]{3,2,1,0:T(4,128)S(1)}, u32[]{:S(2)}, u32[]{:S(2)}) async-start(f32[32,3,4,128]{3,2,1,0:T(4,128)} %get-tuple-element.49), calls=%async_computation | async-start | bytes 393216 | tf_op jit(solution)/shard_map/all_to_all | solution.py:427
  10.7 0.4 copies.1
  11.1 1.8 %collective-permute-start = (f32[32,1152]{1,0:T(8,128)S(1)}, f32[32,1152]{1,0:T(8,128)S(1)}, u32[]{:S(2)}, u32[]{:S(2)}) collective-permute-start(f32[32,1152]{1,0:T(8,128)S(1)} %get-tuple-element.53), channel_id=1, source_target_pairs={{0,8},{16,24},{8,0},{24,16},{1,9},{17,25},{9,1},{25,17},{2,10},{18... | collective-permute-start | bytes 442376 | tf_op jit(solution)/shard_map/ppermute | solution.py:469
  12.9 0.7 collective-permute-start.1
  13.6 0.1 collective-permute-start.2
  13.7 0.7 collective-permute-start.3
  14.4 9.3 %first_local.1 = (bf16[8192,256]{1,0:T(8,128)(2,1)}, bf16[8192,256]{1,0:T(8,128)(2,1)}, f32[8,2048]{1,0:T(8,128)S(1)}, bf16[128,2048]{1,0:T(8,128)(2,1)S(1)}) custom-call(f32[8192,128]{1,0:T(8,128)} %flex_raw.1, f32[8192,128]{1,0:T(8,128)} %stiff_raw.1, f32[8,2048]{1,0:T(8,128)S(1)} %get-tuple-element.59.rhs.refs_8_, ...), custom_call_target="tpu_custom_call" | custom-call | tf_op jit(solution)/shard_map/first_local/pallas_call | solution.py:491
  23.6 0.0 collective-permute-done.refs_0_
  23.7 0.0 collective-permute-done.1.refs_1_
  23.7 0.0 collective-permute-done.2.refs_2_
  23.7 0.0 collective-permute-done.3.refs_3_
  23.7 0.6 prepare.1
  24.3 0.0 all-to-all-done.refs_1_
  24.3 2.7 %step0.1 = (f32[32,3,4,128]{3,2,1,0:T(4,128)}, f32[8,2048]{1,0:T(8,128)S(1)}, f32[8,2048]{1,0:T(8,128)S(1)}, f32[8,256]{1,0:T(8,128)S(1)}, f32[8,512]{1,0:T(8,128)S(1)}) custom-call(s32[2]{0:T(128)S(1)} %pad_add_fusion.pos.refs_0_, f32[32,3,4,128]{3,2,1,0:T(4,128)S(1)} %all-to-all-done.refs_1_, bf16[512,1024]{1,0:T(8,128)(2,1)S(1)} %get-tuple-element.57.refs_2_, ...), custom_call_target="tpu_custom_call" | custom-call | tf_op jit(solution)/shard_map/step0/pallas_call | solution.py:540
  26.9 9.2 %all-to-all-start.1 = ((f32[32,3,4,128]{3,2,1,0:T(4,128)}), f32[32,3,4,128]{3,2,1,0:T(4,128)S(1)}, u32[]{:S(2)}, u32[]{:S(2)}) async-start(f32[32,3,4,128]{3,2,1,0:T(4,128)} %get-tuple-element.64), calls=%async_computation.1 | async-start | bytes 393216 | tf_op jit(solution)/shard_map/all_to_all | solution.py:427
  36.1 6.5 %local.2.refs_9_ = f32[8,2048]{1,0:T(8,128)S(1)} custom-call(bf16[8192,256]{1,0:T(8,128)(2,1)} %get-tuple-element.65.flex_held, bf16[8192,256]{1,0:T(8,128)(2,1)} %get-tuple-element.66.stiff_held, f32[8,2048]{1,0:T(8,128)S(1)} %get-tuple-element.67.field.refs_12_, s32[4,16]{1,0:T(4,128)} %bitcast.5, s32[4,16]{1,0:T(4,128)} %bitcast.8), custom_call_target="tpu_custom_call" | custom-call | tf_op jit(solution)/shard_map/local/pallas_call | solution.py:519
  42.6 2.3 %all-to-all-done.1.refs_1_ = f32[32,3,4,128]{3,2,1,0:T(4,128)S(1)} async-done(((f32[32,3,4,128]{3,2,1,0:T(4,128)}), f32[32,3,4,128]{3,2,1,0:T(4,128)S(1)}, u32[]{:S(2)}, u32[]{:S(2)}) %all-to-all-start.1) | async-done | bytes 196640 | tf_op jit(solution)/shard_map/all_to_all | solution.py:427
  44.9 2.7 %step1.1 = (f32[8,2048]{1,0:T(8,128)S(1)}, f32[8,2048]{1,0:T(8,128)S(1)}, f32[8,2048]{1,0:T(8,128)S(1)}, f32[8,2048]{1,0:T(8,128)S(1)}, f32[8,2048]{1,0:T(8,128)...) custom-call(s32[2]{0:T(128)S(1)} %pad_add_fusion.pos.refs_0_, ...), custom_call_target="tpu_custom_call" | custom-call | tf_op jit(solution)/shard_map/step1/pallas_call | solution.py:540
  47.6 3.8 %all-to-all-start.2 = ((f32[32,3,4,128]{3,2,1,0:T(4,128)}), f32[32,3,4,128]{3,2,1,0:T(4,128)S(1)}, u32[]{:S(2)}, u32[]{:S(2)}) async-start(f32[32,3,4,128]{3,2,1,0:T(4,128)} %get-tuple-element.71), calls=%async_computation.2 | async-start | bytes 393216 | tf_op jit(solution)/shard_map/all_to_all | solution.py:427
  51.4 6.5 %local.3.refs_9_ = f32[8,2048]{1,0:T(8,128)S(1)} custom-call(bf16[8192,256]{1,0:T(8,128)(2,1)} %get-tuple-element.65.flex_held, bf16[8192,256]{1,0:T(8,128)(2,1)} %get-tuple-element.66.stiff_held, f32[8,2048]{1,0:T(8,128)S(1)} %get-tuple-element.73.field.refs_12_, s32[4,16]{1,0:T(4,128)} %bitcast.6, s32[4,16]{1,0:T(4,128)} %bitcast.9), custom_call_target="tpu_custom_call" | custom-call | tf_op jit(solution)/shard_map/local/pallas_call | solution.py:519
  57.9 2.1 %all-to-all-done.2.refs_1_ = f32[32,3,4,128]{3,2,1,0:T(4,128)S(1)} async-done(((f32[32,3,4,128]{3,2,1,0:T(4,128)}), f32[32,3,4,128]{3,2,1,0:T(4,128)S(1)}, u32[]{:S(2)}, u32[]{:S(2)}) %all-to-all-start.2) | async-done | bytes 196640 | tf_op jit(solution)/shard_map/all_to_all | solution.py:427
  59.9 2.0 %step2.1 = (f32[8,2048]{1,0:T(8,128)S(1)}, f32[8,2048]{1,0:T(8,128)S(1)}, f32[8,2048]{1,0:T(8,128)S(1)}, f32[8,2048]{1,0:T(8,128)S(1)}, f32[8,2048]{1,0:T(8,128)...) custom-call(s32[2]{0:T(128)S(1)} %pad_add_fusion.pos.refs_0_, ...), custom_call_target="tpu_custom_call" | custom-call | tf_op jit(solution)/shard_map/step2/pallas_call | solution.py:540
  61.9 10.8 %all_to_all.20.refs_1_ = f32[32,1,4,128]{3,2,1,0:T(4,128)S(1)} all-to-all(f32[32,1,4,128]{3,2,1,0:T(4,128)S(1)} %get-tuple-element.85), channel_id=1, replica_groups=mesh['row'=4,'col'=8] {'row','col'}, dimensions={0} | all-to-all | bytes 131072 | tf_op jit(solution)/shard_map/all_to_all | solution.py:427
  72.8 1.8 %step3.1 = (f32[8,2048]{1,0:T(8,128)}, f32[8,2048]{1,0:T(8,128)}, f32[8,2048]{1,0:T(8,128)}) custom-call(s32[2]{0:T(128)S(1)} %pad_add_fusion.pos.refs_0_, f32[32,1,4,128]{3,2,1,0:T(4,128)S(1)} %all_to_all.20.refs_1_, bf16[512,1024]{1,0:T(8,128)(2,1)S(1)} %get-tuple-element.57.refs_2_, bf16[128,2048]{1,0:T(8,128)(2,1)S(1)} %get-tuple-element.58.refs_3_, ...), custom_call_target="tpu_custom_call" | custom-call | tf_op jit(solution)/shard_map/step3/pallas_call | solution.py:540
Async XLA Ops:
  3.4 20.8 %all-to-all-start = ((f32[32,3,4,128]{3,2,1,0:T(4,128)}), f32[32,3,4,128]{3,2,1,0:T(4,128)S(1)}, u32[]{:S(2)}, u32[]{:S(2)}) async-start(f32[32,3,4,128]{3,2,1,0:T(4,128)} %get-tuple-element.49), calls=%async_computation | async-start | bytes 393216 | tf_op jit(solution)/shard_map/all_to_all | solution.py:427
  11.1 12.5 %collective-permute-start = (f32[32,1152]{1,0:T(8,128)S(1)}, f32[32,1152]{1,0:T(8,128)S(1)}, u32[]{:S(2)}, u32[]{:S(2)}) collective-permute-start(f32[32,1152]{1,0:T(8,128)S(1)} %get-tuple-element.53), channel_id=1, source_target_pairs={{0,8},{16,24},{8,0},{24,16},{1,9},{17,25},{9,1},{25,17},{2,10},{18... | collective-permute-start | bytes 442376 | tf_op jit(solution)/shard_map/ppermute | solution.py:469
  12.9 10.7 %collective-permute-start.1 = (f32[32,1152]{1,0:T(8,128)S(1)}, f32[32,1152]{1,0:T(8,128)S(1)}, u32[]{:S(2)}, u32[]{:S(2)}) collective-permute-start(f32[32,1152]{1,0:T(8,128)S(1)} %get-tuple-element.54), channel_id=1, source_target_pairs={{8,16},{16,8},{9,17},{17,9},{10,18},{18,10},{11,19},{19,11},{12,20... | collective-permute-start | bytes 442376 | tf_op jit(solution)/shard_map/ppermute | solution.py:469
  13.6 10.1 %collective-permute-start.2 = (f32[32,1152]{1,0:T(8,128)S(1)}, f32[32,1152]{1,0:T(8,128)S(1)}, u32[]{:S(2)}, u32[]{:S(2)}) collective-permute-start(f32[32,1152]{1,0:T(8,128)S(1)} %get-tuple-element.55), channel_id=1, source_target_pairs={{0,1},{2,3},{4,5},{6,7},{1,0},{3,2},{5,4},{7,6},{8,9},{10,11},{12,... | collective-permute-start | bytes 442376 | tf_op jit(solution)/shard_map/ppermute | solution.py:469
  13.7 10.0 %collective-permute-start.3 = (f32[32,1152]{1,0:T(8,128)S(1)}, f32[32,1152]{1,0:T(8,128)S(1)}, u32[]{:S(2)}, u32[]{:S(2)}) collective-permute-start(f32[32,1152]{1,0:T(8,128)S(1)} %get-tuple-element.56), channel_id=1, source_target_pairs={{1,2},{3,4},{5,6},{2,1},{4,3},{6,5},{9,10},{11,12},{13,14},{10,9},... | collective-permute-start | bytes 442376 | tf_op jit(solution)/shard_map/ppermute | solution.py:469
  26.9 17.9 %all-to-all-start.1 = ((f32[32,3,4,128]{3,2,1,0:T(4,128)}), f32[32,3,4,128]{3,2,1,0:T(4,128)S(1)}, u32[]{:S(2)}, u32[]{:S(2)}) async-start(f32[32,3,4,128]{3,2,1,0:T(4,128)} %get-tuple-element.64), calls=%async_computation.1 | async-start | bytes 393216 | tf_op jit(solution)/shard_map/all_to_all | solution.py:427
  47.6 12.4 %all-to-all-start.2 = ((f32[32,3,4,128]{3,2,1,0:T(4,128)}), f32[32,3,4,128]{3,2,1,0:T(4,128)S(1)}, u32[]{:S(2)}, u32[]{:S(2)}) async-start(f32[32,3,4,128]{3,2,1,0:T(4,128)} %get-tuple-element.71), calls=%async_computation.2 | async-start | bytes 393216 | tf_op jit(solution)/shard_map/all_to_all | solution.py:427
where the time goes:
time: 74.9 us; the launch traced here: 74.5 us
  Pallas kernels  35 us (47%)
  starting transfers between devices  23.5 us (31%)
  blocking collectives  10.8 us (14%)
  waiting for transfers between devices  4.34 us (6%)
  between operations  0.77 us (1%)
    all_to_all x3, starting transfers between devices, exchange(): return lax.all_to_all(slots, AXES, 0, 0)  20.3 us
    pallas_call x2, Pallas kernels, apply_local(): call(local_kernel, held(whole), [HBM] * 2 + [VMEM] + [HBM] * 2, 'local',...  13 us
    all_to_all x1, blocking collectives, exchange(): return lax.all_to_all(slots, AXES, 0, 0)  10.8 us
    pallas_call x1, Pallas kernels, shards(): call(first_local_kernel, (pltpu.HBM(tiles_shape, BF16), pltpu.HBM(tiles_s...  9.28 us
    pallas_call x4, Pallas kernels, step(): call(functools.partial(step_kernel, grid, kind, tuple(state), tuple(outs)...  9.1 us
    all_to_all x3, waiting for transfers between devices, exchange(): return lax.all_to_all(slots, AXES, 0, 0)  4.33 us
    ppermute x4, starting transfers between devices, shards(): lax.ppermute(c, axis, pairs_of(n, odd))  3.23 us
    pallas_call x1, Pallas kernels, shards(): call(functools.partial(lead_kernel, grid), (slots, held((4 * defl, wide),...  2.71 us
  transfers between devices with their start and end apart: 7, of which 2 were waited for; matrix products, arithmetic and copies ran while one was open for 0% of the time, Pallas kernels for 31%

commit v1 on v0

--- a/solution.py
+++ b/solution.py
@@ -120,7 +120,14 @@
 def coefficients(field, basis):
     out = lax.dot_general(stacked(field), basis[...], NT, preferred_element_type=F32)
     out = out[: field.shape[0]] + out[field.shape[0] :]
+    out = jnp.concatenate([out, out], axis=1)
     return out + pltpu.roll(out, LANE // 4, axis=1)
+
+
+def expand(energy, basis):
+    loads = energy.shape[0]
+    out = jnp.dot(stacked(energy[:, : LANE // 2]), basis[...], preferred_element_type=F32)
+    return out[:loads] + out[loads:]
 
 
 def write_slots(slots, packed, traces, sides):
@@ -135,7 +142,8 @@
 
 
 def lead_kernel(grid, pos, *refs):
-    sources, (slots, basis, faces), targets, (lengths, rows, sems) = refs[:5], refs[5:8], refs[8:11], refs[11:]
+    sources, (slots, basis, faces, trace), targets = refs[:5], refs[5:9], refs[9:12]
+    lengths, rows, sems = refs[12:]
     copies = []
     for k, (src, dst) in enumerate(zip(sources, targets + (rows, lengths))):
         copies.append(pltpu.make_async_copy(src, dst, sems.at[k]))
@@ -144,8 +152,7 @@
     for copy in copies:
         copy.wait()
     sides = neighbours(pos, *grid)
-    hi, lo = split(deflation[...])
-    basis[...] = jnp.concatenate([hi, lo, hi, lo], axis=0)
+    basis[...] = stacked(deflation[...])
     field = rhs[...]
     coefs = coefficients(field, basis)
     tiles = tiles_of(field)
@@ -158,29 +165,33 @@
         faces[g : g + 1, :] = index
         faces[g + 4 : g + 5, :] = jnp.where(lane < live, 1, 0)
         traces.append(pick_lanes(tiles, index))
+    trace[...] = jnp.concatenate(traces, axis=1)
     packed = pack(coefs, (), (pos[0] * grid[1] + pos[1]) % 4)
     write_slots(slots, packed, traces, sides)
 
 
-def copies_kernel(deflation, coarse, faces, *outs):
+def copies_kernel(deflation, coarse, faces, *refs):
+    outs, face_basis = refs[:4], refs[4]
     wide = coarse.shape[1]
     tiles = tiles_of(deflation[...])
     for g, out in enumerate(outs):
         out[:, :wide] = coarse[...]
-        out[:, wide:] = pick_lanes(tiles, faces[g : g + 1, :])
+        at_face = pick_lanes(tiles, faces[g : g + 1, :])
+        out[:, wide:] = at_face
+        face_basis[:, g * LANE : (g + 1) * LANE] = stacked(at_face)
 
 
 def prepare_kernel(coarse, faces, *refs):
     received, (weights, partner_basis, inverse) = refs[:4], refs[4:]
     wide = coarse.shape[1]
     defl = coarse.shape[0]
-    weights_own = split(coarse[...])
+    own = split(coarse[...])
+    for k, part in enumerate((own[0], own[0], own[1], own[1])):
+        weights[LANE + k * defl : LANE + (k + 1) * defl, :] = part
     partner_basis[...] = jnp.zeros_like(partner_basis)
     for g, ref in enumerate(received):
         for half, part in enumerate(split(ref[:, :wide])):
-            weights[half * 256 + g * defl : half * 256 + (g + 1) * defl, :] = part
-        for half, part in enumerate(weights_own):
-            at = half * 256 + LANE + g * defl
+            at = 2 * half * LANE + g * defl
             weights[at : at + defl, :] = part
         for half, part in enumerate(split(ref[:, wide:])):
             at = half * LANE + g * defl
@@ -228,12 +239,7 @@
         dst[b] = jnp.concatenate(parts, axis=0)
 
 
-PARTS = 4
-
-
-def block_of(tiles, per_row):
-    deep = per_row * LANE
-    return lambda b: tiles[b * deep : (b + 1) * deep, :]
+PARTS = 2
 
 
 def transfer(source, target, sems, parts=1):
@@ -251,78 +257,80 @@
         copy.wait()
 
 
-def first_local_kernel(
-    flex_raw, stiff_raw, rhs, deflation, flex_list, stiff_list,
-    flex_out, stiff_out, local, local_basis,
-    first, second, total, raw_first, raw_second, flex, stiff, flex_cols, stiff_cols, sems,
-):
-    per_row, blocks = flex_cols.shape
+def joined(after, jumps, inverse):
+    pieces = tiles_of(jumps)
+    out = []
+    for b, tile in enumerate(tiles_of(after)):
+        code = inverse[b : b + 1, :]
+        out.append(tile + pick_lanes(pieces, jnp.where(code < 0, jumps.shape[1], code)))
+    return out
+
+
+def join_kernel(after, jumps, inverse, out):
+    out[...] = jnp.concatenate(joined(after[...], jumps[...], inverse), axis=1)
+
+
+def apply_tiles(lists, arriving, raw, tiles, cols, spaces, rows):
+    first, second, total = spaces
+    per_row, blocks = cols[0].shape
     deep = per_row * LANE
-    arriving = (
-        transfer(flex_raw, raw_first, sems.at[0], PARTS),
-        transfer(stiff_raw, raw_second, sems.at[1], PARTS),
+
+    def block(s):
+        return lambda b: tiles[s][b * deep : (b + 1) * deep, :]
+
+    def converted(s):
+        def get(b):
+            if b % (blocks // PARTS) == 0:
+                arriving[s][b // (blocks // PARTS)].wait()
+            at = slice(b * deep, (b + 1) * deep)
+            hi, lo = split(raw[s][at, :])
+            tiles[s][at, :LANE] = hi
+            tiles[s][at, LANE:] = lo
+            return block(s)(b)
+
+        return get
+
+    wait(lists)
+    forward(cols[0], converted(0), first, second, rows)
+    forward(cols[1], converted(1), second, first, rows)
+    backward(cols[1], block(1), first, total, rows)
+    restack(total, second, rows)
+    backward(cols[0], block(0), second, total, rows)
+
+
+def begin(sources, lists, raw, cols, sems):
+    return (
+        transfer(lists[0], cols[0], sems.at[2]) + transfer(lists[1], cols[1], sems.at[3]),
+        [transfer(sources[s], raw[s], sems.at[s], PARTS) for s in range(2)],
     )
-    lists = transfer(flex_list, flex_cols, sems.at[2]) + transfer(stiff_list, stiff_cols, sems.at[3])
+
+
+def first_local_kernel(flex, stiff, flex_list, stiff_list, rhs, deflation, local, local_basis, *scratch):
+    spaces, raw, tiles, cols, sems = scratch[:3], scratch[3:5], scratch[5:7], scratch[7:9], scratch[9]
+    lists, arriving = begin((flex, stiff), (flex_list, stiff_list), raw, cols, sems)
+    first, total = spaces[0], spaces[2]
     loads, defl = rhs.shape[0], deflation.shape[0]
-    rows = ((0, loads), (2 * loads, defl))
-    for b in range(blocks):
+    for b in range(first.shape[0]):
         at = slice(b * LANE, (b + 1) * LANE)
         first[b] = jnp.concatenate([stacked(rhs[:, at]), stacked(deflation[:, at])], axis=0)
-
-    def convert(raw, out, b):
-        hi, lo = split(raw[b * deep : (b + 1) * deep, :])
-        out[b * deep : (b + 1) * deep, :LANE] = hi
-        out[b * deep : (b + 1) * deep, LANE:] = lo
-
-    def converted(raw, out):
-        def tiles(b):
-            convert(raw, out, b)
-            return block_of(out, per_row)(b)
-
-        return tiles
-
-    wait(lists)
-    for copy in arriving[0]:
-        copy.wait()
-    forward(flex_cols, converted(raw_first, flex), first, second, rows)
-    leaving = transfer(flex, flex_out, sems.at[2], PARTS)
-    for copy in arriving[1]:
-        copy.wait()
-    forward(stiff_cols, converted(raw_second, stiff), second, first, rows)
-    leaving += transfer(stiff, stiff_out, sems.at[3], PARTS)
-    backward(stiff_cols, block_of(stiff, per_row), first, total, rows)
-    restack(total, second, rows)
-    backward(flex_cols, block_of(flex, per_row), second, total, rows)
-    for b in range(blocks):
+    apply_tiles(lists, arriving, raw, tiles, cols, spaces, ((0, loads), (2 * loads, defl)))
+    for b in range(first.shape[0]):
         at = slice(b * LANE, (b + 1) * LANE)
         local[:, at] = total[b][:loads]
-        hi, lo = split(total[b][loads:])
-        local_basis[:, at] = jnp.concatenate([hi, lo, hi, lo], axis=0)
-    wait(leaving)
+        local_basis[:, at] = stacked(total[b][loads:])
 
 
 def local_kernel(
-    flex_held, stiff_held, field, flex_list, stiff_list,
-    local, first, second, total, flex, stiff, flex_cols, stiff_cols, sems,
+    flex, stiff, flex_list, stiff_list, after, jumps, inverse, out, local, *scratch
 ):
-    per_row, blocks = flex_cols.shape
-    lists = transfer(flex_list, flex_cols, sems.at[2]) + transfer(stiff_list, stiff_cols, sems.at[3])
-    arriving = (
-        transfer(flex_held, flex, sems.at[0], PARTS),
-        transfer(stiff_held, stiff, sems.at[1], PARTS),
-    )
-    rows = ((0, field.shape[0]),)
-    for b in range(blocks):
-        first[b] = stacked(field[:, b * LANE : (b + 1) * LANE])
-    wait(lists)
-    wait(arriving[0])
-    forward(flex_cols, block_of(flex, per_row), first, second, rows)
-    wait(arriving[1])
-    forward(stiff_cols, block_of(stiff, per_row), second, first, rows)
-    backward(stiff_cols, block_of(stiff, per_row), first, total, rows)
-    restack(total, second, rows)
-    backward(flex_cols, block_of(flex, per_row), second, total, rows)
-    for b in range(blocks):
+    spaces, raw, tiles, cols, sems = scratch[:3], scratch[3:5], scratch[5:7], scratch[7:9], scratch[9]
+    lists, arriving = begin((flex, stiff), (flex_list, stiff_list), raw, cols, sems)
+    first, total = spaces[0], spaces[2]
+    for b, tile in enumerate(joined(after[...], jumps[...], inverse)):
+        out[:, b * LANE : (b + 1) * LANE] = tile
+        first[b] = stacked(tile)
+    apply_tiles(lists, arriving, raw, tiles, cols, spaces, ((0, after.shape[0]),))
+    for b in range(first.shape[0]):
         local[:, b * LANE : (b + 1) * LANE] = total[b]
 
 
@@ -338,7 +346,10 @@
     coefs, dots = unpack(lambda s: received[s, last], count, loads)
     both = lax.dot_general(stacked(coefs), old.weights[...], NT, preferred_element_type=F32)
     both = both[:loads] + both[loads:]
-    energy = both[:, :256] + both[:, 256:]
+    own = both[:, LANE : 2 * LANE]
+    energy = jnp.concatenate(
+        [both[:, :LANE] + both[:, 2 * LANE :], own + pltpu.roll(own, LANE // 2, axis=1)], axis=1
+    )
 
     def partner_traces():
         traces = []
@@ -351,11 +362,13 @@
     if kind == START:
         residual, local_residual = old.residual[...], old.local_after[...]
         energy_residual, partner_residual = energy, partner_traces()
+        trace_residual = old.trace_after[...]
     else:
         if kind == FIRST:
             curvature, descent = dots[0], dots[1]
             direction, image, energy_image = old.correction[...], old.after[...], energy
             local_image, partner_image = old.local_after[...], partner_traces()
+            trace_image = old.trace_after[...]
         else:
             energy_sum, project_sum, cross_sum, old_sum = dots
             before = jnp.max(old.curvature[...], axis=1, keepdims=True)
@@ -368,6 +381,7 @@
             if kind == MIDDLE:
                 local_image = old.local_after[...] + blend * old.local_image[...]
                 partner_image = partner_traces() + blend * old.partner_image[...]
+                trace_image = old.trace_after[...] + blend * old.trace_image[...]
         step = descent / curvature
         residual = old.residual[...] - step * image
         energy_residual = old.energy_residual[...] - step * energy_image
@@ -377,47 +391,42 @@
         if kind != LAST:
             local_residual = old.local_residual[...] - step * local_image
             partner_residual = old.partner_residual[...] - step * partner_image
-            keep.update(local_image=local_image, partner_image=partner_image)
+            trace_residual = old.trace_residual[...] - step * trace_image
+            keep.update(local_image=local_image, partner_image=partner_image, trace_image=trace_image)
     keep.update(energy_residual=energy_residual)
 
     own = energy_residual[:, LANE:]
-    hi, lo = split(own)
-    lane = iota(own.shape, 1)
-    lhs = jnp.where(lane < LANE // 2, hi.astype(F32), lo.astype(F32)).astype(BF16)
-    correction = residual + jnp.dot(lhs, old.basis[...], preferred_element_type=F32)
+    correction = residual + expand(own, old.basis)
     keep.update(correction=correction)
     if kind != LAST:
-        local = local_residual + jnp.dot(lhs, old.local_basis[...], preferred_element_type=F32)
+        local = local_residual + expand(own, old.local_basis)
         hi, lo = split(energy_residual[:, :LANE])
         pairs = jnp.concatenate(
             [jnp.concatenate([hi, hi], axis=1), jnp.concatenate([lo, lo], axis=1)], axis=0
         )
         other = jnp.dot(pairs, old.partner_basis[...], preferred_element_type=F32)
         partner = partner_residual + other[:loads] + other[loads:]
-        faces, inverse = old.faces, old.inverse
-        tiles = tiles_of(correction)
-        jumps = []
-        for g in range(4):
-            trace = pick_lanes(tiles, faces[g : g + 1, :])
-            jump = trace - partner[:, g * LANE : (g + 1) * LANE]
-            jumps.append(jnp.where(faces[g + 4 : g + 5, :] > 0, jump, 0.0))
-        pieces = []
-        for b in range(len(tiles)):
-            code = inverse[b : b + 1, :]
-            pieces.append(pick_lanes(jumps, jnp.where(code < 0, 4 * LANE, code)))
-        after = correction + local + jnp.concatenate(pieces, axis=1)
+        trace = trace_residual + expand(own, old.face_basis)
+        faces = old.faces
+        live = jnp.concatenate([faces[g + 4 : g + 5, :] for g in range(4)], axis=1)
+        jumps = jnp.where(live > 0, trace - partner, 0.0)
+        after = correction + local
 
         dot = lambda a, b: jnp.sum(a * b, axis=1, keepdims=True)
-        sums = [dot(correction, after), dot(residual, correction)]
+        sums = [dot(correction, after) + dot(trace, jumps), dot(residual, correction)]
         if kind != START:
             sums += [dot(correction, image), dot(residual, direction)]
-        packed = pack(coefficients(after, old.basis), sums, (pos[0] * grid[1] + pos[1]) % 4)
+        coefs = coefficients(after, old.basis) + coefficients(jumps, old.face_basis)
+        packed = pack(coefs, sums, (pos[0] * grid[1] + pos[1]) % 4)
         traces = []
         if kind != MIDDLE:
             tiles = tiles_of(after)
             traces = [pick_lanes(tiles, faces[g : g + 1, :]) for g in range(4)]
+            traces = [t + j for t, j in zip(traces, tiles_of(jumps))]
+            keep.update(trace_after=jnp.concatenate(traces, axis=1))
         write_slots(out.slots, packed, traces, sides)
-        keep.update(after=after, partner_residual=partner_residual, local_residual=local_residual)
+        keep.update(after=after, jumps=jumps, trace_residual=trace_residual)
+        keep.update(partner_residual=partner_residual, local_residual=local_residual)
     for k, v in keep.items():
         if hasattr(out, k):
             getattr(out, k)[...] = v
@@ -443,13 +452,16 @@
     whole = (loads, wide)
     slots = held((count, 3, 4, LANE))
 
-    slots_now, basis, faces, rhs, deflation, coarse_rows = call(
+    field, energy, traces = held(whole), held((loads, 256)), held((loads, 4 * LANE))
+
+    slots_now, basis, faces, trace, rhs, deflation, coarse_rows = call(
         functools.partial(lead_kernel, grid),
         (
             slots,
-            held((4 * defl, wide), BF16),
+            held((2 * defl, wide), BF16),
             held((8, LANE), I32),
-            held(whole),
+            traces,
+            field,
             held(deflation.shape),
             held(coarse_rows.shape),
         ),
@@ -459,9 +471,9 @@
     )(pos, *in_hbm(rhs, deflation, coarse_rows, face_rows, face_len))
     received = exchange(slots_now)
 
-    copies = call(
+    *copies, face_basis = call(
         copies_kernel,
-        (jax.ShapeDtypeStruct((defl, coarse + LANE), F32),) * 4,
+        (jax.ShapeDtypeStruct((defl, coarse + LANE), F32),) * 4 + (held((2 * defl, 4 * LANE), BF16),),
         [VMEM, VMEM, VMEM],
         "copies",
     )(deflation, coarse_rows, faces)
@@ -471,54 +483,39 @@
             copies, (("row", grid[0], 0), ("row", grid[0], 1), ("col", grid[1], 0), ("col", grid[1], 1))
         )
     ]
-    lists = in_hbm(flex_cols.T, stiff_cols.T)
-    tiles_shape = (flex_tiles.shape[0], 2 * LANE)
-    tile_scratch = (
-        pltpu.VMEM(tiles_shape, BF16),
-        pltpu.VMEM(tiles_shape, BF16),
-        pltpu.SMEM((per_row, blocks), I32),
-        pltpu.SMEM((per_row, blocks), I32),
-        pltpu.SemaphoreType.DMA((4, PARTS)),
-    )
-
-    def block_scratch(rows):
+    lists = in_hbm(flex_tiles, stiff_tiles, flex_cols.T, stiff_cols.T)
+
+    def scratch(rows):
         return (
-            pltpu.VMEM((blocks, 2 * rows, LANE), BF16),
-            pltpu.VMEM((blocks, 2 * rows, LANE), BF16),
-            pltpu.VMEM((blocks, rows, LANE), F32),
+            (pltpu.VMEM((blocks, 2 * rows, LANE), BF16),) * 2
+            + (pltpu.VMEM((blocks, rows, LANE), F32),)
+            + (pltpu.VMEM(flex_tiles.shape, F32),) * 2
+            + (pltpu.VMEM((flex_tiles.shape[0], 2 * LANE), BF16),) * 2
+            + (pltpu.SMEM((per_row, blocks), I32),) * 2
+            + (pltpu.SemaphoreType.DMA((4, PARTS)),)
         )
 
-    flex, stiff, local, local_basis = call(
+    local, local_basis = call(
         first_local_kernel,
-        (
-            pltpu.HBM(tiles_shape, BF16),
-            pltpu.HBM(tiles_shape, BF16),
-            held(whole),
-            held((4 * defl, wide), BF16),
-        ),
-        [HBM] * 2 + [VMEM] * 2 + [HBM] * 2,
+        (field, held((2 * defl, wide), BF16)),
+        [HBM] * 4 + [VMEM] * 2,
         "first_local",
-        scratch=block_scratch(loads + defl)
-        + (pltpu.VMEM(flex_tiles.shape, F32), pltpu.VMEM(stiff_tiles.shape, F32))
-        + tile_scratch,
-        out_specs=(HBM, HBM, VMEM, VMEM),
-    )(
-        *in_hbm(flex_tiles, stiff_tiles),
-        rhs,
-        deflation,
-        *lists,
-    )
+        scratch(loads + defl),
+    )(*lists, rhs, deflation)
     weights, partner_basis, inverse = call(
         prepare_kernel,
-        (held((512, coarse), BF16), held((2 * LANE, 4 * LANE), BF16), held((blocks, LANE), I32)),
+        (held((3 * LANE, coarse), BF16), held((2 * LANE, 4 * LANE), BF16), held((blocks, LANE), I32)),
         [VMEM] * 6,
         "prepare",
     )(coarse_rows, faces, *copies)
 
-    def apply_local(field):
-        return call(
-            local_kernel, held(whole), [HBM] * 2 + [VMEM] + [HBM] * 2, "local", block_scratch(loads) + tile_scratch
-        )(*in_hbm(flex, stiff), field, *lists)
+    def apply_local(after, jumps):
+        return call(local_kernel, (field, field), [HBM] * 4 + [VMEM] * 3, "local", scratch(loads))(
+            *lists, after, jumps, inverse
+        )
+
+    def join(after, jumps):
+        return call(join_kernel, field, [VMEM] * 3, "join")(after, jumps, inverse)
 
     state = dict(
         pos=pos,
@@ -528,12 +525,12 @@
         local_basis=local_basis,
         partner_basis=partner_basis,
         faces=faces,
-        inverse=inverse,
+        face_basis=face_basis,
         residual=rhs,
+        trace_after=trace,
         local_after=local,
         local_residual=local,
     )
-    field, energy, traces = held(whole), held((loads, 256)), held((loads, 4 * LANE))
     result = jax.ShapeDtypeStruct(whole, F32)
 
     def step(kind, **outs):
@@ -546,18 +543,23 @@
         state.update(zip(outs, done))
 
     step(
-        START, slots=slots, correction=field, after=field, energy_residual=energy, partner_residual=traces
+        START, slots=slots, correction=field, after=field, jumps=traces, energy_residual=energy,
+        partner_residual=traces, trace_after=traces, trace_residual=traces,
     )
     for iteration in range(ITERS):
         state.update(received=exchange(state.pop("slots")))
+        pair = state["after"], state.pop("jumps")
         if iteration + 1 < ITERS:
-            state.update(local_after=apply_local(state["after"]))
+            state.update(zip(("after", "local_after"), apply_local(*pair)))
+        else:
+            state.update(after=join(*pair))
         kept = dict(
             solution=field, residual=field, correction=field, direction=field, image=field, after=field,
-            energy_residual=energy, energy_image=energy, curvature=held((loads, LANE)), slots=slots,
+            jumps=traces, energy_residual=energy, energy_image=energy, curvature=held((loads, LANE)), slots=slots,
         )
         more = dict(
-            partner_residual=traces, local_residual=field, partner_image=traces, local_image=field
+            partner_residual=traces, local_residual=field, partner_image=traces, local_image=field,
+            trace_residual=traces, trace_image=traces, trace_after=traces,
         )
         if iteration + 1 == ITERS:
             step(LAST, solution=result, residual=result, correction=result)

time: 74.9 us -> 72.5 us (0.968)
  blocking collectives: 10.8 us -> 0 us
  waiting for transfers between devices: 4.34 us -> 11.5 us
  starting transfers between devices: 23.5 us -> 27.1 us
  Pallas kernels: 35 us -> 32.5 us
    all_to_all x1 -> x0, blocking collectives: 10.8 us -> none  [exchange(): return lax.all_to_all(slots, AXES, 0, 0)]
    all_to_all x3 -> x4, waiting for transfers between devices: 4.33 us -> 11.5 us  [exchange(): return lax.all_to_all(slots, AXES, 0, 0)]
    all_to_all x3 -> x4, starting transfers between devices: 20.3 us -> 23.9 us  [exchange(): return lax.all_to_all(slots, AXES, 0, 0)]
    pallas_call x5 -> x6, Pallas kernels: 25.5 us -> 23.6 us  [the longest x2 13 us: apply_local(): call(local_kernel, (field, field), [HBM] * 4 + [VMEM] * 3, 'local', scrat...]
  transfers between devices with their start and end apart: 7 -> 8, of which waited for: 2 -> 3; matrix products, arithmetic and copies ran while one was open for 0% -> 0% of each run, Pallas kernels for 31% -> 30%
where the time goes in v1:
time: 72.5 us; the launch traced here: 72 us
  Pallas kernels  32.5 us (45%)
  starting transfers between devices  27.1 us (37%)
  waiting for transfers between devices  11.5 us (16%)
  between operations  0.78 us (1%)
    all_to_all x4, starting transfers between devices, exchange(): return lax.all_to_all(slots, AXES, 0, 0)  23.9 us
    pallas_call x2, Pallas kernels, apply_local(): call(local_kernel, (field, field), [HBM] * 4 + [VMEM] * 3, 'local', scrat...  13 us
    all_to_all x4, waiting for transfers between devices, exchange(): return lax.all_to_all(slots, AXES, 0, 0)  11.5 us
    pallas_call x4, Pallas kernels, step(): call(functools.partial(step_kernel, grid, kind, tuple(state), tuple(outs)...  8.5 us
    pallas_call x1, Pallas kernels, shards(): call(first_local_kernel, (field, held((2 * defl, wide), BF16)), [HBM] * 4...  7.28 us
    ppermute x4, starting transfers between devices, shards(): lax.ppermute(c, axis, pairs_of(n, odd))  3.23 us
    pallas_call x1, Pallas kernels, shards(): call(functools.partial(lead_kernel, grid), (slots, held((2 * defl, wide),...  2.64 us
  transfers between devices with their start and end apart: 8, of which 3 were waited for; matrix products, arithmetic and copies ran while one was open for 0% of the time, Pallas kernels for 30%

profile of v1, /device:TPU:0, one launch (start us, length us, event | category | flops | bytes accessed | tf_op | source)
XLA Modules:
  0.0 72.0 jit_solution(2571726664913440789)
XLA Ops:
  0.6 0.1 pad_add_fusion.pos.refs_0_
  0.7 2.6 %lead.1 = (f32[32,3,4,128]{3,2,1,0:T(4,128)}, bf16[64,2048]{1,0:T(8,128)(2,1)S(1)}, s32[8,128]{1,0:T(8,128)S(1)}, f32[8,512]{1,0:T(8,128)S(1)}, f32[8,2048]{1,0:...) custom-call(s32[2]{0:T(128)S(1)} %pad_add_fusion.pos.refs_0_, f32[8,2048]{1,0:T(8,128)} %refs_0_.1, ...), custom_call_target="tpu_custom_call" | custom-call | tf_op jit(solution)/shard_map/lead/pallas_call | solution.py:457
  3.4 7.3 %all-to-all-start = ((f32[32,3,4,128]{3,2,1,0:T(4,128)}), f32[32,3,4,128]{3,2,1,0:T(4,128)S(1)}, u32[]{:S(2)}, u32[]{:S(2)}) async-start(f32[32,3,4,128]{3,2,1,0:T(4,128)} %get-tuple-element.61), calls=%async_computation | async-start | bytes 393216 | tf_op jit(solution)/shard_map/all_to_all | solution.py:436
  10.7 0.4 copies.1
  11.0 1.8 %collective-permute-start = (f32[32,1152]{1,0:T(8,128)S(1)}, f32[32,1152]{1,0:T(8,128)S(1)}, u32[]{:S(2)}, u32[]{:S(2)}) collective-permute-start(f32[32,1152]{1,0:T(8,128)S(1)} %get-tuple-element.65), channel_id=1, source_target_pairs={{0,8},{16,24},{8,0},{24,16},{1,9},{17,25},{9,1},{25,17},{2,10},{18... | collective-permute-start | bytes 442376 | tf_op jit(solution)/shard_map/ppermute | solution.py:481
  12.9 0.7 collective-permute-start.1
  13.5 0.1 collective-permute-start.2
  13.6 0.7 collective-permute-start.3
  14.3 7.3 %first_local.1 = (f32[8,2048]{1,0:T(8,128)S(1)}, bf16[64,2048]{1,0:T(8,128)(2,1)S(1)}) custom-call(f32[8192,128]{1,0:T(8,128)} %flex.5, f32[8192,128]{1,0:T(8,128)} %stiff.5, s32[4,16]{1,0:T(4,128)} %bitcast.4, s32[4,16]{1,0:T(4,128)} %bitcast.7, f32[8,2048]{1,0:T(8,128)S(1)} %get-tuple-element.71.rhs.refs_8_, f32[32,2048]{1,0:T(8,128)S(1)} %get-tuple-element.64.deflation), custom_call_target="tpu_custom_call" | custom-call | tf_op jit(solution)/shard_map/first_local/pallas_call | solution.py:498
  21.6 0.0 collective-permute-done.refs_0_
  21.6 0.0 collective-permute-done.1.refs_1_
  21.6 0.0 collective-permute-done.2.refs_2_
  21.6 0.0 collective-permute-done.3.refs_3_
  21.6 0.6 prepare.1
  22.2 0.0 all-to-all-done.refs_1_
  22.2 2.3 %step0.1 = (f32[32,3,4,128]{3,2,1,0:T(4,128)}, f32[8,2048]{1,0:T(8,128)S(1)}, f32[8,2048]{1,0:T(8,128)S(1)}, f32[8,512]{1,0:T(8,128)S(1)}, f32[8,256]{1,0:T(8,12...) custom-call(s32[2]{0:T(128)S(1)} %pad_add_fusion.pos.refs_0_, ...), custom_call_target="tpu_custom_call" | custom-call | tf_op jit(solution)/shard_map/step0/pallas_call | solution.py:537
  24.5 9.1 %all-to-all-start.1 = ((f32[32,3,4,128]{3,2,1,0:T(4,128)}), f32[32,3,4,128]{3,2,1,0:T(4,128)S(1)}, u32[]{:S(2)}, u32[]{:S(2)}) async-start(f32[32,3,4,128]{3,2,1,0:T(4,128)} %get-tuple-element.77), calls=%async_computation.1 | async-start | bytes 393216 | tf_op jit(solution)/shard_map/all_to_all | solution.py:436
  33.6 6.5 %local.2 = (f32[8,2048]{1,0:T(8,128)S(1)}, f32[8,2048]{1,0:T(8,128)S(1)}) custom-call(f32[8192,128]{1,0:T(8,128)} %flex.5, f32[8192,128]{1,0:T(8,128)} %stiff.5, s32[4,16]{1,0:T(4,128)} %bitcast.5, s32[4,16]{1,0:T(4,128)} %bitcast.8, f32[8,2048]{1,0:T(8,128)S(1)} %get-tuple-element.79.after, f32[8,512]{1,0:T(8,128)S(1)} %get-tuple-element.80.jumps, ...), custom_call_target="tpu_custom_call" | custom-call | tf_op jit(solution)/shard_map/local/pallas_call | solution.py:513
  40.1 2.3 %all-to-all-done.1.refs_1_ = f32[32,3,4,128]{3,2,1,0:T(4,128)S(1)} async-done(((f32[32,3,4,128]{3,2,1,0:T(4,128)}), f32[32,3,4,128]{3,2,1,0:T(4,128)S(1)}, u32[]{:S(2)}, u32[]{:S(2)}) %all-to-all-start.1) | async-done | bytes 196640 | tf_op jit(solution)/shard_map/all_to_all | solution.py:436
  42.4 2.3 %step1.1 = (f32[8,2048]{1,0:T(8,128)S(1)}, f32[8,2048]{1,0:T(8,128)S(1)}, f32[8,2048]{1,0:T(8,128)S(1)}, f32[8,2048]{1,0:T(8,128)S(1)}, f32[8,2048]{1,0:T(8,128)...) custom-call(s32[2]{0:T(128)S(1)} %pad_add_fusion.pos.refs_0_, ...), custom_call_target="tpu_custom_call" | custom-call | tf_op jit(solution)/shard_map/step1/pallas_call | solution.py:537
  44.6 3.8 %all-to-all-start.2 = ((f32[32,3,4,128]{3,2,1,0:T(4,128)}), f32[32,3,4,128]{3,2,1,0:T(4,128)S(1)}, u32[]{:S(2)}, u32[]{:S(2)}) async-start(f32[32,3,4,128]{3,2,1,0:T(4,128)} %get-tuple-element.88), calls=%async_computation.2 | async-start | bytes 393216 | tf_op jit(solution)/shard_map/all_to_all | solution.py:436
  48.5 6.5 %local.3 = (f32[8,2048]{1,0:T(8,128)S(1)}, f32[8,2048]{1,0:T(8,128)S(1)}) custom-call(f32[8192,128]{1,0:T(8,128)} %flex.5, f32[8192,128]{1,0:T(8,128)} %stiff.5, s32[4,16]{1,0:T(4,128)} %bitcast.6, s32[4,16]{1,0:T(4,128)} %bitcast.9, f32[8,2048]{1,0:T(8,128)S(1)} %get-tuple-element.91.after, f32[8,512]{1,0:T(8,128)S(1)} %get-tuple-element.92.jumps, ...), custom_call_target="tpu_custom_call" | custom-call | tf_op jit(solution)/shard_map/local/pallas_call | solution.py:513
  54.9 2.1 %all-to-all-done.2.refs_1_ = f32[32,3,4,128]{3,2,1,0:T(4,128)S(1)} async-done(((f32[32,3,4,128]{3,2,1,0:T(4,128)}), f32[32,3,4,128]{3,2,1,0:T(4,128)S(1)}, u32[]{:S(2)}, u32[]{:S(2)}) %all-to-all-start.2) | async-done | bytes 196640 | tf_op jit(solution)/shard_map/all_to_all | solution.py:436
  57.0 2.2 %step2.1 = (f32[8,2048]{1,0:T(8,128)S(1)}, f32[8,2048]{1,0:T(8,128)S(1)}, f32[8,2048]{1,0:T(8,128)S(1)}, f32[8,2048]{1,0:T(8,128)S(1)}, f32[8,2048]{1,0:T(8,128)...) custom-call(s32[2]{0:T(128)S(1)} %pad_add_fusion.pos.refs_0_, ...), custom_call_target="tpu_custom_call" | custom-call | tf_op jit(solution)/shard_map/step2/pallas_call | solution.py:537
  59.2 3.6 %all-to-all-start.3 = ((f32[32,1,4,128]{3,2,1,0:T(4,128)}), f32[32,1,4,128]{3,2,1,0:T(4,128)S(1)}, u32[]{:S(2)}, u32[]{:S(2)}) async-start(f32[32,1,4,128]{3,2,1,0:T(4,128)} %get-tuple-element.108), calls=%async_computation.3 | async-start | bytes 131072 | tf_op jit(solution)/shard_map/all_to_all | solution.py:436
  62.9 0.2 join.1.refs_13_
  63.1 7.2 %all-to-all-done.3.refs_1_ = f32[32,1,4,128]{3,2,1,0:T(4,128)S(1)} async-done(((f32[32,1,4,128]{3,2,1,0:T(4,128)}), f32[32,1,4,128]{3,2,1,0:T(4,128)S(1)}, u32[]{:S(2)}, u32[]{:S(2)}) %all-to-all-start.3) | async-done | bytes 65568 | tf_op jit(solution)/shard_map/all_to_all | solution.py:436
  70.3 1.8 %step3.1 = (f32[8,2048]{1,0:T(8,128)}, f32[8,2048]{1,0:T(8,128)}, f32[8,2048]{1,0:T(8,128)}) custom-call(s32[2]{0:T(128)S(1)} %pad_add_fusion.pos.refs_0_, f32[32,1,4,128]{3,2,1,0:T(4,128)S(1)} %all-to-all-done.3.refs_1_, bf16[384,1024]{1,0:T(8,128)(2,1)S(1)} %get-tuple-element.69.refs_2_, bf16[64,2048]{1,0:T(8,128)(2,1)S(1)} %get-tuple-element.70.refs_3_, ...), custom_call_target="tpu_custom_call" | custom-call | tf_op jit(solution)/shard_map/step3/pallas_call | solution.py:537
Async XLA Ops:
  3.4 18.8 %all-to-all-start = ((f32[32,3,4,128]{3,2,1,0:T(4,128)}), f32[32,3,4,128]{3,2,1,0:T(4,128)S(1)}, u32[]{:S(2)}, u32[]{:S(2)}) async-start(f32[32,3,4,128]{3,2,1,0:T(4,128)} %get-tuple-element.61), calls=%async_computation | async-start | bytes 393216 | tf_op jit(solution)/shard_map/all_to_all | solution.py:436
  11.0 10.5 %collective-permute-start = (f32[32,1152]{1,0:T(8,128)S(1)}, f32[32,1152]{1,0:T(8,128)S(1)}, u32[]{:S(2)}, u32[]{:S(2)}) collective-permute-start(f32[32,1152]{1,0:T(8,128)S(1)} %get-tuple-element.65), channel_id=1, source_target_pairs={{0,8},{16,24},{8,0},{24,16},{1,9},{17,25},{9,1},{25,17},{2,10},{18... | collective-permute-start | bytes 442376 | tf_op jit(solution)/shard_map/ppermute | solution.py:481
  12.9 8.7 %collective-permute-start.1 = (f32[32,1152]{1,0:T(8,128)S(1)}, f32[32,1152]{1,0:T(8,128)S(1)}, u32[]{:S(2)}, u32[]{:S(2)}) collective-permute-start(f32[32,1152]{1,0:T(8,128)S(1)} %get-tuple-element.66), channel_id=1, source_target_pairs={{8,16},{16,8},{9,17},{17,9},{10,18},{18,10},{11,19},{19,11},{12,20... | collective-permute-start | bytes 442376 | tf_op jit(solution)/shard_map/ppermute | solution.py:481
  13.5 8.1 %collective-permute-start.2 = (f32[32,1152]{1,0:T(8,128)S(1)}, f32[32,1152]{1,0:T(8,128)S(1)}, u32[]{:S(2)}, u32[]{:S(2)}) collective-permute-start(f32[32,1152]{1,0:T(8,128)S(1)} %get-tuple-element.67), channel_id=1, source_target_pairs={{0,1},{2,3},{4,5},{6,7},{1,0},{3,2},{5,4},{7,6},{8,9},{10,11},{12,... | collective-permute-start | bytes 442376 | tf_op jit(solution)/shard_map/ppermute | solution.py:481
  13.6 8.0 %collective-permute-start.3 = (f32[32,1152]{1,0:T(8,128)S(1)}, f32[32,1152]{1,0:T(8,128)S(1)}, u32[]{:S(2)}, u32[]{:S(2)}) collective-permute-start(f32[32,1152]{1,0:T(8,128)S(1)} %get-tuple-element.68), channel_id=1, source_target_pairs={{1,2},{3,4},{5,6},{2,1},{4,3},{6,5},{9,10},{11,12},{13,14},{10,9},... | collective-permute-start | bytes 442376 | tf_op jit(solution)/shard_map/ppermute | solution.py:481
  24.5 17.9 %all-to-all-start.1 = ((f32[32,3,4,128]{3,2,1,0:T(4,128)}), f32[32,3,4,128]{3,2,1,0:T(4,128)S(1)}, u32[]{:S(2)}, u32[]{:S(2)}) async-start(f32[32,3,4,128]{3,2,1,0:T(4,128)} %get-tuple-element.77), calls=%async_computation.1 | async-start | bytes 393216 | tf_op jit(solution)/shard_map/all_to_all | solution.py:436
  44.6 12.4 %all-to-all-start.2 = ((f32[32,3,4,128]{3,2,1,0:T(4,128)}), f32[32,3,4,128]{3,2,1,0:T(4,128)S(1)}, u32[]{:S(2)}, u32[]{:S(2)}) async-start(f32[32,3,4,128]{3,2,1,0:T(4,128)} %get-tuple-element.88), calls=%async_computation.2 | async-start | bytes 393216 | tf_op jit(solution)/shard_map/all_to_all | solution.py:436
  59.2 11.0 %all-to-all-start.3 = ((f32[32,1,4,128]{3,2,1,0:T(4,128)}), f32[32,1,4,128]{3,2,1,0:T(4,128)S(1)}, u32[]{:S(2)}, u32[]{:S(2)}) async-start(f32[32,1,4,128]{3,2,1,0:T(4,128)} %get-tuple-element.108), calls=%async_computation.3 | async-start | bytes 131072 | tf_op jit(solution)/shard_map/all_to_all | solution.py:436

commit v2 on v1

--- a/solution.py
+++ b/solution.py
@@ -182,7 +182,8 @@
 
 
 def prepare_kernel(coarse, faces, *refs):
-    received, (weights, partner_basis, inverse) = refs[:4], refs[4:]
+    received, (weights, partner_basis, named) = refs[:4], refs[4:]
+    named[...] = find_slots(faces, named.shape[0])
     wide = coarse.shape[1]
     defl = coarse.shape[0]
     own = split(coarse[...])
@@ -196,17 +197,6 @@
         for half, part in enumerate(split(ref[:, wide:])):
             at = half * LANE + g * defl
             partner_basis[at : at + defl, g * LANE : (g + 1) * LANE] = part
-    columns = [
-        jnp.transpose(jnp.broadcast_to(faces[g : g + 1, :].astype(F32), (LANE, LANE)))
-        for g in range(4)
-    ]
-    slot, lane = iota((LANE, LANE), 0), iota((LANE, LANE), 1)
-    for b in range(inverse.shape[0]):
-        found = jnp.zeros((LANE, LANE), F32)
-        here = (lane + b * LANE).astype(F32)
-        for g in range(4):
-            found = jnp.where(columns[g] == here, (slot + (g * LANE + 1)).astype(F32), found)
-        inverse[b : b + 1, :] = jnp.sum(found, axis=0, keepdims=True).astype(I32) - 1
 
 
 def forward(cols, tiles, src, dst, rows):
@@ -239,14 +229,14 @@
         dst[b] = jnp.concatenate(parts, axis=0)
 
 
-PARTS = 2
-
-
-def transfer(source, target, sems, parts=1):
-    step = source.shape[0] // parts
+def parts_of(blocks):
+    return ((0, blocks // 2), (blocks // 2, blocks))
+
+
+def transfer(source, target, sems, parts=None):
     copies = []
-    for k in range(parts):
-        at = pl.ds(k * step, step)
+    for k, (low, high) in enumerate(parts or ((0, source.shape[0]),)):
+        at = pl.ds(low, high - low)
         copies.append(pltpu.make_async_copy(source.at[at], target.at[at], sems.at[k]))
         copies[-1].start()
     return copies
@@ -257,17 +247,32 @@
         copy.wait()
 
 
-def joined(after, jumps, inverse):
+def find_slots(faces, blocks):
+    lists = faces[0:4, :]
+    names = jnp.concatenate([lists[g : g + 1, :] for g in range(4)], axis=1)
+    row, slot = iota((blocks, 4 * LANE), 0), iota((blocks, 4 * LANE), 1)
+    here = names // LANE == row
+    at = jnp.where(here, (slot % LANE).astype(F32), 0.0)
+    face = jnp.where(here, (slot // LANE + 1).astype(F32), 0.0)
+    lane = iota((LANE, LANE), 1).astype(F32)
+    found = []
+    for g in range(4):
+        column = jnp.transpose(jnp.broadcast_to((lists[g : g + 1, :] % LANE).astype(F32), (LANE, LANE)))
+        found.append(jnp.where(column == lane, 1.0, 0.0))
+    both = jnp.dot(
+        jnp.concatenate([at, face], axis=0).astype(BF16),
+        jnp.concatenate(found, axis=0).astype(BF16),
+        preferred_element_type=F32,
+    )
+    at, face = both[:blocks].astype(I32), both[blocks:].astype(I32)
+    return jnp.where(face > 0, (face - 1) * LANE + at, 4 * LANE)
+
+
+def joined(after, jumps, slots):
     pieces = tiles_of(jumps)
-    out = []
-    for b, tile in enumerate(tiles_of(after)):
-        code = inverse[b : b + 1, :]
-        out.append(tile + pick_lanes(pieces, jnp.where(code < 0, jumps.shape[1], code)))
-    return out
-
-
-def join_kernel(after, jumps, inverse, out):
-    out[...] = jnp.concatenate(joined(after[...], jumps[...], inverse), axis=1)
+    return [
+        tile + pick_lanes(pieces, slots[b : b + 1, :]) for b, tile in enumerate(tiles_of(after))
+    ]
 
 
 def apply_tiles(lists, arriving, raw, tiles, cols, spaces, rows):
@@ -280,8 +285,9 @@
 
     def converted(s):
         def get(b):
-            if b % (blocks // PARTS) == 0:
-                arriving[s][b // (blocks // PARTS)].wait()
+            for copy, (low, _) in zip(arriving[s], parts_of(blocks)):
+                if b == low:
+                    copy.wait()
             at = slice(b * deep, (b + 1) * deep)
             hi, lo = split(raw[s][at, :])
             tiles[s][at, :LANE] = hi
@@ -299,9 +305,11 @@
 
 
 def begin(sources, lists, raw, cols, sems):
+    per_row, blocks = lists[0].shape
+    parts = [(low * per_row * LANE, high * per_row * LANE) for low, high in parts_of(blocks)]
     return (
         transfer(lists[0], cols[0], sems.at[2]) + transfer(lists[1], cols[1], sems.at[3]),
-        [transfer(sources[s], raw[s], sems.at[s], PARTS) for s in range(2)],
+        [transfer(sources[s], raw[s], sems.at[s], parts) for s in range(2)],
     )
 
 
@@ -321,12 +329,12 @@
 
 
 def local_kernel(
-    flex, stiff, flex_list, stiff_list, after, jumps, inverse, out, local, *scratch
+    flex, stiff, flex_list, stiff_list, after, jumps, named, out, local, *scratch
 ):
     spaces, raw, tiles, cols, sems = scratch[:3], scratch[3:5], scratch[5:7], scratch[7:9], scratch[9]
     lists, arriving = begin((flex, stiff), (flex_list, stiff_list), raw, cols, sems)
     first, total = spaces[0], spaces[2]
-    for b, tile in enumerate(joined(after[...], jumps[...], inverse)):
+    for b, tile in enumerate(joined(after[...], jumps[...], named)):
         out[:, b * LANE : (b + 1) * LANE] = tile
         first[b] = stacked(tile)
     apply_tiles(lists, arriving, raw, tiles, cols, spaces, ((0, after.shape[0]),))
@@ -334,9 +342,18 @@
         local[:, b * LANE : (b + 1) * LANE] = total[b]
 
 
+def update(dots, curvature):
+    energy_sum, project_sum, cross_sum, old_sum = dots
+    before = jnp.max(curvature[...], axis=1, keepdims=True)
+    blend = -cross_sum / before
+    after = energy_sum + 2.0 * blend * cross_sum + blend * blend * before
+    return after, project_sum + blend * old_sum, blend
+
+
 def step_kernel(grid, kind, names, out_names, *refs):
     old = SimpleNamespace(**dict(zip(names, refs)))
-    out = SimpleNamespace(**dict(zip(out_names, refs[len(names) :])))
+    done = len(names) + len(out_names)
+    out = SimpleNamespace(**dict(zip(out_names, refs[len(names) : done])))
     pos, received = old.pos, old.received
     loads = old.residual.shape[0]
     count = received.shape[0]
@@ -344,6 +361,21 @@
     sides = neighbours(pos, *grid)
 
     coefs, dots = unpack(lambda s: received[s, last], count, loads)
+    leaving = []
+
+    def send(k, value, target):
+        refs[done + k][...] = value
+        leaving.append(pltpu.make_async_copy(refs[done + k], target, refs[-1].at[k]))
+        leaving[-1].start()
+
+    if kind == LAST:
+        curvature, descent, blend = update(dots, old.curvature)
+        step = descent / curvature
+        direction = old.correction[...] + blend * old.direction[...]
+        send(0, old.solution[...] + step * direction, out.solution)
+        residual = old.residual[...] - step * (old.after[...] + blend * old.image[...])
+        send(1, residual, out.residual)
+
     both = lax.dot_general(stacked(coefs), old.weights[...], NT, preferred_element_type=F32)
     both = both[:loads] + both[loads:]
     own = both[:, LANE : 2 * LANE]
@@ -357,6 +389,13 @@
             trace = jnp.concatenate([received[device, 0], received[device, 1]], axis=0)
             traces.append(jnp.where(there, trace, 0.0))
         return jnp.concatenate(traces, axis=1)
+
+    if kind == LAST:
+        energy = energy[:, LANE:] + blend * old.energy_image[:, LANE:]
+        own = old.energy_residual[:, LANE:] - step * energy
+        send(2, residual + expand(own, old.basis), out.correction)
+        wait(leaving)
+        return
 
     keep = {}
     if kind == START:
@@ -370,63 +409,58 @@
             local_image, partner_image = old.local_after[...], partner_traces()
             trace_image = old.trace_after[...]
         else:
-            energy_sum, project_sum, cross_sum, old_sum = dots
-            before = jnp.max(old.curvature[...], axis=1, keepdims=True)
-            blend = -cross_sum / before
-            curvature = energy_sum + 2.0 * blend * cross_sum + blend * blend * before
-            descent = project_sum + blend * old_sum
+            curvature, descent, blend = update(dots, old.curvature)
             direction = old.correction[...] + blend * old.direction[...]
             image = old.after[...] + blend * old.image[...]
             energy_image = energy + blend * old.energy_image[...]
-            if kind == MIDDLE:
-                local_image = old.local_after[...] + blend * old.local_image[...]
-                partner_image = partner_traces() + blend * old.partner_image[...]
-                trace_image = old.trace_after[...] + blend * old.trace_image[...]
+            local_image = old.local_after[...] + blend * old.local_image[...]
+            partner_image = partner_traces() + blend * old.partner_image[...]
+            trace_image = old.trace_after[...] + blend * old.trace_image[...]
         step = descent / curvature
         residual = old.residual[...] - step * image
         energy_residual = old.energy_residual[...] - step * energy_image
         out.solution[...] = step * direction + (0.0 if kind == FIRST else old.solution[...])
         keep.update(residual=residual, direction=direction, image=image, energy_image=energy_image)
         keep.update(curvature=jnp.broadcast_to(curvature, (loads, LANE)))
-        if kind != LAST:
-            local_residual = old.local_residual[...] - step * local_image
-            partner_residual = old.partner_residual[...] - step * partner_image
-            trace_residual = old.trace_residual[...] - step * trace_image
-            keep.update(local_image=local_image, partner_image=partner_image, trace_image=trace_image)
+        local_residual = old.local_residual[...] - step * local_image
+        partner_residual = old.partner_residual[...] - step * partner_image
+        trace_residual = old.trace_residual[...] - step * trace_image
+        keep.update(local_image=local_image, partner_image=partner_image, trace_image=trace_image)
     keep.update(energy_residual=energy_residual)
 
     own = energy_residual[:, LANE:]
+    hi, lo = split(energy_residual[:, :LANE])
+    pairs = jnp.concatenate(
+        [jnp.concatenate([hi, hi], axis=1), jnp.concatenate([lo, lo], axis=1)], axis=0
+    )
+    other = jnp.dot(pairs, old.partner_basis[...], preferred_element_type=F32)
+    partner = partner_residual + other[:loads] + other[loads:]
+    trace = trace_residual + expand(own, old.face_basis)
+    faces = old.faces
+    live = jnp.concatenate([faces[g + 4 : g + 5, :] for g in range(4)], axis=1)
+    jumps = jnp.where(live > 0, trace - partner, 0.0)
     correction = residual + expand(own, old.basis)
     keep.update(correction=correction)
-    if kind != LAST:
-        local = local_residual + expand(own, old.local_basis)
-        hi, lo = split(energy_residual[:, :LANE])
-        pairs = jnp.concatenate(
-            [jnp.concatenate([hi, hi], axis=1), jnp.concatenate([lo, lo], axis=1)], axis=0
-        )
-        other = jnp.dot(pairs, old.partner_basis[...], preferred_element_type=F32)
-        partner = partner_residual + other[:loads] + other[loads:]
-        trace = trace_residual + expand(own, old.face_basis)
-        faces = old.faces
-        live = jnp.concatenate([faces[g + 4 : g + 5, :] for g in range(4)], axis=1)
-        jumps = jnp.where(live > 0, trace - partner, 0.0)
-        after = correction + local
-
-        dot = lambda a, b: jnp.sum(a * b, axis=1, keepdims=True)
-        sums = [dot(correction, after) + dot(trace, jumps), dot(residual, correction)]
-        if kind != START:
-            sums += [dot(correction, image), dot(residual, direction)]
-        coefs = coefficients(after, old.basis) + coefficients(jumps, old.face_basis)
-        packed = pack(coefs, sums, (pos[0] * grid[1] + pos[1]) % 4)
-        traces = []
-        if kind != MIDDLE:
-            tiles = tiles_of(after)
-            traces = [pick_lanes(tiles, faces[g : g + 1, :]) for g in range(4)]
-            traces = [t + j for t, j in zip(traces, tiles_of(jumps))]
-            keep.update(trace_after=jnp.concatenate(traces, axis=1))
-        write_slots(out.slots, packed, traces, sides)
-        keep.update(after=after, jumps=jumps, trace_residual=trace_residual)
-        keep.update(partner_residual=partner_residual, local_residual=local_residual)
+    local = local_residual + expand(own, old.local_basis)
+    after = correction + local
+
+    dot = lambda a, b: jnp.sum(a * b, axis=1, keepdims=True)
+    sums = [dot(correction, after) + dot(trace, jumps), dot(residual, correction)]
+    if kind != START:
+        sums += [dot(correction, image), dot(residual, direction)]
+    coefs = coefficients(after, old.basis) + coefficients(jumps, old.face_basis)
+    packed = pack(coefs, sums, (pos[0] * grid[1] + pos[1]) % 4)
+    traces = []
+    if kind != MIDDLE:
+        tiles = tiles_of(after)
+        traces = [pick_lanes(tiles, faces[g : g + 1, :]) for g in range(4)]
+        traces = [t + j for t, j in zip(traces, tiles_of(jumps))]
+        keep.update(trace_after=jnp.concatenate(traces, axis=1))
+    write_slots(out.slots, packed, traces, sides)
+    if kind == MIDDLE:
+        after = jnp.concatenate(joined(after, jumps, old.named), axis=1)
+    keep.update(after=after, jumps=jumps, trace_residual=trace_residual)
+    keep.update(partner_residual=partner_residual, local_residual=local_residual)
     for k, v in keep.items():
         if hasattr(out, k):
             getattr(out, k)[...] = v
@@ -492,7 +526,7 @@
             + (pltpu.VMEM(flex_tiles.shape, F32),) * 2
             + (pltpu.VMEM((flex_tiles.shape[0], 2 * LANE), BF16),) * 2
             + (pltpu.SMEM((per_row, blocks), I32),) * 2
-            + (pltpu.SemaphoreType.DMA((4, PARTS)),)
+            + (pltpu.SemaphoreType.DMA((4, 2)),)
         )
 
     local, local_basis = call(
@@ -502,7 +536,7 @@
         "first_local",
         scratch(loads + defl),
     )(*lists, rhs, deflation)
-    weights, partner_basis, inverse = call(
+    weights, partner_basis, named = call(
         prepare_kernel,
         (held((3 * LANE, coarse), BF16), held((2 * LANE, 4 * LANE), BF16), held((blocks, LANE), I32)),
         [VMEM] * 6,
@@ -511,11 +545,8 @@
 
     def apply_local(after, jumps):
         return call(local_kernel, (field, field), [HBM] * 4 + [VMEM] * 3, "local", scratch(loads))(
-            *lists, after, jumps, inverse
+            *lists, after, jumps, named
         )
-
-    def join(after, jumps):
-        return call(join_kernel, field, [VMEM] * 3, "join")(after, jumps, inverse)
 
     state = dict(
         pos=pos,
@@ -526,6 +557,7 @@
         partner_basis=partner_basis,
         faces=faces,
         face_basis=face_basis,
+        named=named,
         residual=rhs,
         trace_after=trace,
         local_after=local,
@@ -534,11 +566,14 @@
     result = jax.ShapeDtypeStruct(whole, F32)
 
     def step(kind, **outs):
+        last = kind == LAST
         done = call(
             functools.partial(step_kernel, grid, kind, tuple(state), tuple(outs)),
             tuple(outs.values()),
             [SMEM] + [VMEM] * (len(state) - 1),
             f"step{kind}",
+            (pltpu.VMEM(whole, F32),) * 3 + (pltpu.SemaphoreType.DMA((3,)),) if last else (),
+            (HBM,) * 3 if last else None,
         )(*state.values())
         state.update(zip(outs, done))
 
@@ -548,11 +583,9 @@
     )
     for iteration in range(ITERS):
         state.update(received=exchange(state.pop("slots")))
-        pair = state["after"], state.pop("jumps")
         if iteration + 1 < ITERS:
-            state.update(zip(("after", "local_after"), apply_local(*pair)))
-        else:
-            state.update(after=join(*pair))
+            pair = apply_local(state["after"], state.pop("jumps"))
+            state.update(zip(("after", "local_after"), pair))
         kept = dict(
             solution=field, residual=field, correction=field, direction=field, image=field, after=field,
             jumps=traces, energy_residual=energy, energy_image=energy, curvature=held((loads, LANE)), slots=slots,
@@ -567,6 +600,7 @@
             step(FIRST, **kept, **more)
         else:
             kept.update(slots=held((count, 1, 4, LANE)))
+            kept.pop("jumps")
             step(MIDDLE, **kept)
     return state["solution"], state["residual"], state["correction"]
 

time: 72.5 us -> 71.7 us (0.989)
  blocking collectives: 0 us -> 10.8 us
  waiting for transfers between devices: 11.5 us -> 4.35 us
  starting transfers between devices: 27.1 us -> 23.5 us
  Pallas kernels: 32.5 us -> 31.5 us
    all_to_all x0 -> x1, blocking collectives: none -> 10.8 us  [exchange(): return lax.all_to_all(slots, AXES, 0, 0)]
    all_to_all x4 -> x3, waiting for transfers between devices: 11.5 us -> 4.34 us  [exchange(): return lax.all_to_all(slots, AXES, 0, 0)]
    all_to_all x4 -> x3, starting transfers between devices: 23.9 us -> 20.3 us  [exchange(): return lax.all_to_all(slots, AXES, 0, 0)]
  transfers between devices with their start and end apart: 8 -> 7, of which waited for: 3 -> 2; matrix products, arithmetic and copies ran while one was open for 0% -> 0% of each run, Pallas kernels for 30% -> 29%
where the time goes in v2:
time: 71.7 us; the launch traced here: 71.2 us
  Pallas kernels  31.5 us (44%)
  starting transfers between devices  23.5 us (33%)
  blocking collectives  10.8 us (15%)
  waiting for transfers between devices  4.35 us (6%)
  between operations  0.93 us (1%)
    all_to_all x3, starting transfers between devices, exchange(): return lax.all_to_all(slots, AXES, 0, 0)  20.3 us
    pallas_call x2, Pallas kernels, apply_local(): call(local_kernel, (field, field), [HBM] * 4 + [VMEM] * 3, 'local', scrat...  13 us
    all_to_all x1, blocking collectives, exchange(): return lax.all_to_all(slots, AXES, 0, 0)  10.8 us
    pallas_call x4, Pallas kernels, step(): call(functools.partial(step_kernel, grid, kind, tuple(state), tuple(outs)...  7.94 us
    pallas_call x1, Pallas kernels, shards(): call(first_local_kernel, (field, held((2 * defl, wide), BF16)), [HBM] * 4...  7.27 us
    all_to_all x3, waiting for transfers between devices, exchange(): return lax.all_to_all(slots, AXES, 0, 0)  4.34 us
    ppermute x4, starting transfers between devices, shards(): lax.ppermute(c, axis, pairs_of(n, odd))  3.23 us
    pallas_call x1, Pallas kernels, shards(): call(functools.partial(lead_kernel, grid), (slots, held((2 * defl, wide),...  2.67 us
  transfers between devices with their start and end apart: 7, of which 2 were waited for; matrix products, arithmetic and copies ran while one was open for 0% of the time, Pallas kernels for 29%

profile of v2, /device:TPU:0, one launch (start us, length us, event | category | flops | bytes accessed | tf_op | source)
XLA Modules:
  0.0 71.2 jit_solution(15814724760383068900)
XLA Ops:
  0.6 0.1 pad_add_fusion.pos.refs_0_
  0.7 2.7 %lead.1 = (f32[32,3,4,128]{3,2,1,0:T(4,128)}, bf16[64,2048]{1,0:T(8,128)(2,1)S(1)}, s32[8,128]{1,0:T(8,128)S(1)}, f32[8,512]{1,0:T(8,128)S(1)}, f32[8,2048]{1,0:...) custom-call(s32[2]{0:T(128)S(1)} %pad_add_fusion.pos.refs_0_, f32[8,2048]{1,0:T(8,128)} %refs_0_.1, ...), custom_call_target="tpu_custom_call" | custom-call | tf_op jit(solution)/shard_map/lead/pallas_call | solution.py:491
  3.4 7.3 %all-to-all-start = ((f32[32,3,4,128]{3,2,1,0:T(4,128)}), f32[32,3,4,128]{3,2,1,0:T(4,128)S(1)}, u32[]{:S(2)}, u32[]{:S(2)}) async-start(f32[32,3,4,128]{3,2,1,0:T(4,128)} %get-tuple-element.60), calls=%async_computation | async-start | bytes 393216 | tf_op jit(solution)/shard_map/all_to_all | solution.py:470
  10.7 0.4 copies.1
  11.1 1.8 %collective-permute-start = (f32[32,1152]{1,0:T(8,128)S(1)}, f32[32,1152]{1,0:T(8,128)S(1)}, u32[]{:S(2)}, u32[]{:S(2)}) collective-permute-start(f32[32,1152]{1,0:T(8,128)S(1)} %get-tuple-element.64), channel_id=1, source_target_pairs={{0,8},{16,24},{8,0},{24,16},{1,9},{17,25},{9,1},{25,17},{2,10},{18... | collective-permute-start | bytes 442376 | tf_op jit(solution)/shard_map/ppermute | solution.py:515
  12.9 0.7 collective-permute-start.1
  13.6 0.1 collective-permute-start.2
  13.6 0.7 collective-permute-start.3
  14.3 7.3 %first_local.1 = (f32[8,2048]{1,0:T(8,128)S(1)}, bf16[64,2048]{1,0:T(8,128)(2,1)S(1)}) custom-call(f32[8192,128]{1,0:T(8,128)} %flex.5, f32[8192,128]{1,0:T(8,128)} %stiff.5, s32[4,16]{1,0:T(4,128)} %bitcast.4, s32[4,16]{1,0:T(4,128)} %bitcast.7, f32[8,2048]{1,0:T(8,128)S(1)} %get-tuple-element.70.rhs.refs_9_, f32[32,2048]{1,0:T(8,128)S(1)} %get-tuple-element.63.deflation), custom_call_target="tpu_custom_call" | custom-call | tf_op jit(solution)/shard_map/first_local/pallas_call | solution.py:532
  21.6 0.0 collective-permute-done.refs_0_
  21.6 0.0 collective-permute-done.1.refs_1_
  21.6 0.0 collective-permute-done.2.refs_2_
  21.6 0.0 collective-permute-done.3.refs_3_
  21.6 0.3 prepare.1
  22.0 0.0 all-to-all-done.refs_1_
  22.0 2.3 %step0.1 = (f32[32,3,4,128]{3,2,1,0:T(4,128)}, f32[8,2048]{1,0:T(8,128)S(1)}, f32[8,2048]{1,0:T(8,128)S(1)}, f32[8,512]{1,0:T(8,128)S(1)}, f32[8,256]{1,0:T(8,12...) custom-call(s32[2]{0:T(128)S(1)} %pad_add_fusion.pos.refs_0_, ...), custom_call_target="tpu_custom_call" | custom-call | tf_op jit(solution)/shard_map/step0/pallas_call | solution.py:570
  24.2 9.2 %all-to-all-start.1 = ((f32[32,3,4,128]{3,2,1,0:T(4,128)}), f32[32,3,4,128]{3,2,1,0:T(4,128)S(1)}, u32[]{:S(2)}, u32[]{:S(2)}) async-start(f32[32,3,4,128]{3,2,1,0:T(4,128)} %get-tuple-element.77), calls=%async_computation.1 | async-start | bytes 393216 | tf_op jit(solution)/shard_map/all_to_all | solution.py:470
  33.4 6.5 %local.2 = (f32[8,2048]{1,0:T(8,128)S(1)}, f32[8,2048]{1,0:T(8,128)S(1)}) custom-call(f32[8192,128]{1,0:T(8,128)} %flex.5, f32[8192,128]{1,0:T(8,128)} %stiff.5, s32[4,16]{1,0:T(4,128)} %bitcast.5, s32[4,16]{1,0:T(4,128)} %bitcast.8, f32[8,2048]{1,0:T(8,128)S(1)} %get-tuple-element.79.after, f32[8,512]{1,0:T(8,128)S(1)} %get-tuple-element.80.jumps, ...), custom_call_target="tpu_custom_call" | custom-call | tf_op jit(solution)/shard_map/local/pallas_call | solution.py:547
  39.9 2.3 %all-to-all-done.1.refs_1_ = f32[32,3,4,128]{3,2,1,0:T(4,128)S(1)} async-done(((f32[32,3,4,128]{3,2,1,0:T(4,128)}), f32[32,3,4,128]{3,2,1,0:T(4,128)S(1)}, u32[]{:S(2)}, u32[]{:S(2)}) %all-to-all-start.1) | async-done | bytes 196640 | tf_op jit(solution)/shard_map/all_to_all | solution.py:470
  42.2 2.3 %step1.1 = (f32[8,2048]{1,0:T(8,128)S(1)}, f32[8,2048]{1,0:T(8,128)S(1)}, f32[8,2048]{1,0:T(8,128)S(1)}, f32[8,2048]{1,0:T(8,128)S(1)}, f32[8,2048]{1,0:T(8,128)...) custom-call(s32[2]{0:T(128)S(1)} %pad_add_fusion.pos.refs_0_, ...), custom_call_target="tpu_custom_call" | custom-call | tf_op jit(solution)/shard_map/step1/pallas_call | solution.py:570
  44.5 3.8 %all-to-all-start.2 = ((f32[32,3,4,128]{3,2,1,0:T(4,128)}), f32[32,3,4,128]{3,2,1,0:T(4,128)S(1)}, u32[]{:S(2)}, u32[]{:S(2)}) async-start(f32[32,3,4,128]{3,2,1,0:T(4,128)} %get-tuple-element.87), calls=%async_computation.2 | async-start | bytes 393216 | tf_op jit(solution)/shard_map/all_to_all | solution.py:470
  48.3 6.5 %local.3 = (f32[8,2048]{1,0:T(8,128)S(1)}, f32[8,2048]{1,0:T(8,128)S(1)}) custom-call(f32[8192,128]{1,0:T(8,128)} %flex.5, f32[8192,128]{1,0:T(8,128)} %stiff.5, s32[4,16]{1,0:T(4,128)} %bitcast.6, s32[4,16]{1,0:T(4,128)} %bitcast.9, f32[8,2048]{1,0:T(8,128)S(1)} %get-tuple-element.90.after, f32[8,512]{1,0:T(8,128)S(1)} %get-tuple-element.91.jumps, ...), custom_call_target="tpu_custom_call" | custom-call | tf_op jit(solution)/shard_map/local/pallas_call | solution.py:547
  54.8 2.1 %all-to-all-done.2.refs_1_ = f32[32,3,4,128]{3,2,1,0:T(4,128)S(1)} async-done(((f32[32,3,4,128]{3,2,1,0:T(4,128)}), f32[32,3,4,128]{3,2,1,0:T(4,128)S(1)}, u32[]{:S(2)}, u32[]{:S(2)}) %all-to-all-start.2) | async-done | bytes 196640 | tf_op jit(solution)/shard_map/all_to_all | solution.py:470
  56.9 1.6 %step2.1 = (f32[8,2048]{1,0:T(8,128)S(1)}, f32[8,2048]{1,0:T(8,128)S(1)}, f32[8,2048]{1,0:T(8,128)S(1)}, f32[8,2048]{1,0:T(8,128)S(1)}, f32[8,2048]{1,0:T(8,128)...) custom-call(s32[2]{0:T(128)S(1)} %pad_add_fusion.pos.refs_0_, ...), custom_call_target="tpu_custom_call" | custom-call | tf_op jit(solution)/shard_map/step2/pallas_call | solution.py:570
  58.4 10.8 %all_to_all.20.refs_1_ = f32[32,1,4,128]{3,2,1,0:T(4,128)S(1)} all-to-all(f32[32,1,4,128]{3,2,1,0:T(4,128)S(1)} %get-tuple-element.107), channel_id=1, replica_groups=mesh['row'=4,'col'=8] {'row','col'}, dimensions={0} | all-to-all | bytes 131072 | tf_op jit(solution)/shard_map/all_to_all | solution.py:470
  69.3 1.8 %step3.1 = (f32[8,2048]{1,0:T(8,128)}, f32[8,2048]{1,0:T(8,128)}, f32[8,2048]{1,0:T(8,128)}) custom-call(s32[2]{0:T(128)S(1)} %pad_add_fusion.pos.refs_0_, f32[32,1,4,128]{3,2,1,0:T(4,128)S(1)} %all_to_all.20.refs_1_, bf16[384,1024]{1,0:T(8,128)(2,1)S(1)} %get-tuple-element.68.refs_2_, bf16[64,2048]{1,0:T(8,128)(2,1)S(1)} %get-tuple-element.69.refs_3_, ...), custom_call_target="tpu_custom_call" | custom-call | tf_op jit(solution)/shard_map/step3/pallas_call | solution.py:570
Async XLA Ops:
  3.4 18.6 %all-to-all-start = ((f32[32,3,4,128]{3,2,1,0:T(4,128)}), f32[32,3,4,128]{3,2,1,0:T(4,128)S(1)}, u32[]{:S(2)}, u32[]{:S(2)}) async-start(f32[32,3,4,128]{3,2,1,0:T(4,128)} %get-tuple-element.60), calls=%async_computation | async-start | bytes 393216 | tf_op jit(solution)/shard_map/all_to_all | solution.py:470
  11.1 10.5 %collective-permute-start = (f32[32,1152]{1,0:T(8,128)S(1)}, f32[32,1152]{1,0:T(8,128)S(1)}, u32[]{:S(2)}, u32[]{:S(2)}) collective-permute-start(f32[32,1152]{1,0:T(8,128)S(1)} %get-tuple-element.64), channel_id=1, source_target_pairs={{0,8},{16,24},{8,0},{24,16},{1,9},{17,25},{9,1},{25,17},{2,10},{18... | collective-permute-start | bytes 442376 | tf_op jit(solution)/shard_map/ppermute | solution.py:515
  12.9 8.7 %collective-permute-start.1 = (f32[32,1152]{1,0:T(8,128)S(1)}, f32[32,1152]{1,0:T(8,128)S(1)}, u32[]{:S(2)}, u32[]{:S(2)}) collective-permute-start(f32[32,1152]{1,0:T(8,128)S(1)} %get-tuple-element.65), channel_id=1, source_target_pairs={{8,16},{16,8},{9,17},{17,9},{10,18},{18,10},{11,19},{19,11},{12,20... | collective-permute-start | bytes 442376 | tf_op jit(solution)/shard_map/ppermute | solution.py:515
  13.6 8.1 %collective-permute-start.2 = (f32[32,1152]{1,0:T(8,128)S(1)}, f32[32,1152]{1,0:T(8,128)S(1)}, u32[]{:S(2)}, u32[]{:S(2)}) collective-permute-start(f32[32,1152]{1,0:T(8,128)S(1)} %get-tuple-element.66), channel_id=1, source_target_pairs={{0,1},{2,3},{4,5},{6,7},{1,0},{3,2},{5,4},{7,6},{8,9},{10,11},{12,... | collective-permute-start | bytes 442376 | tf_op jit(solution)/shard_map/ppermute | solution.py:515
  13.6 8.0 %collective-permute-start.3 = (f32[32,1152]{1,0:T(8,128)S(1)}, f32[32,1152]{1,0:T(8,128)S(1)}, u32[]{:S(2)}, u32[]{:S(2)}) collective-permute-start(f32[32,1152]{1,0:T(8,128)S(1)} %get-tuple-element.67), channel_id=1, source_target_pairs={{1,2},{3,4},{5,6},{2,1},{4,3},{6,5},{9,10},{11,12},{13,14},{10,9},... | collective-permute-start | bytes 442376 | tf_op jit(solution)/shard_map/ppermute | solution.py:515
  24.2 17.9 %all-to-all-start.1 = ((f32[32,3,4,128]{3,2,1,0:T(4,128)}), f32[32,3,4,128]{3,2,1,0:T(4,128)S(1)}, u32[]{:S(2)}, u32[]{:S(2)}) async-start(f32[32,3,4,128]{3,2,1,0:T(4,128)} %get-tuple-element.77), calls=%async_computation.1 | async-start | bytes 393216 | tf_op jit(solution)/shard_map/all_to_all | solution.py:470
  44.5 12.4 %all-to-all-start.2 = ((f32[32,3,4,128]{3,2,1,0:T(4,128)}), f32[32,3,4,128]{3,2,1,0:T(4,128)S(1)}, u32[]{:S(2)}, u32[]{:S(2)}) async-start(f32[32,3,4,128]{3,2,1,0:T(4,128)} %get-tuple-element.87), calls=%async_computation.2 | async-start | bytes 393216 | tf_op jit(solution)/shard_map/all_to_all | solution.py:470

commit v3 on v2

--- a/solution.py
+++ b/solution.py
@@ -11,6 +11,7 @@
 ITERS = 3
 START, FIRST, MIDDLE, LAST = range(4)
 LANE = 128
+KEPT = 8
 AXES = ("row", "col")
 F32, BF16, I32 = jnp.float32, jnp.bfloat16, jnp.int32
 NT = (((1,), (1,)), ((), ()))
@@ -181,9 +182,8 @@
         face_basis[:, g * LANE : (g + 1) * LANE] = stacked(at_face)
 
 
-def prepare_kernel(coarse, faces, *refs):
-    received, (weights, partner_basis, named) = refs[:4], refs[4:]
-    named[...] = find_slots(faces, named.shape[0])
+def prepare_kernel(coarse, *refs):
+    received, (weights, partner_basis) = refs[:4], refs[4:]
     wide = coarse.shape[1]
     defl = coarse.shape[0]
     own = split(coarse[...])
@@ -229,8 +229,8 @@
         dst[b] = jnp.concatenate(parts, axis=0)
 
 
-def parts_of(blocks):
-    return ((0, blocks // 2), (blocks // 2, blocks))
+def parts_of(blocks, known=0):
+    return ((known, blocks // 2), (blocks // 2, blocks))
 
 
 def transfer(source, target, sems, parts=None):
@@ -275,23 +275,30 @@
     ]
 
 
-def apply_tiles(lists, arriving, raw, tiles, cols, spaces, rows):
+def apply_tiles(lists, arriving, raw, tiles, cols, spaces, rows, kept=None):
     first, second, total = spaces
     per_row, blocks = cols[0].shape
     deep = per_row * LANE
 
+    known = kept.shape[0] // deep if kept is not None else 0
+
     def block(s):
-        return lambda b: tiles[s][b * deep : (b + 1) * deep, :]
+        def get(b):
+            source = kept if s == 0 and b < known else tiles[s]
+            return source[b * deep : (b + 1) * deep, :]
+
+        return get
 
     def converted(s):
         def get(b):
-            for copy, (low, _) in zip(arriving[s], parts_of(blocks)):
+            for copy, (low, _) in zip(arriving[s], parts_of(blocks, known if s == 0 else 0)):
                 if b == low:
                     copy.wait()
-            at = slice(b * deep, (b + 1) * deep)
-            hi, lo = split(raw[s][at, :])
-            tiles[s][at, :LANE] = hi
-            tiles[s][at, LANE:] = lo
+            if s == 1 or b >= known:
+                at = slice(b * deep, (b + 1) * deep)
+                hi, lo = split(raw[s][at, :])
+                tiles[s][at, :LANE] = hi
+                tiles[s][at, LANE:] = lo
             return block(s)(b)
 
         return get
@@ -304,20 +311,27 @@
     backward(cols[0], block(0), second, total, rows)
 
 
-def begin(sources, lists, raw, cols, sems):
+def begin(sources, lists, raw, cols, sems, known=0):
     per_row, blocks = lists[0].shape
-    parts = [(low * per_row * LANE, high * per_row * LANE) for low, high in parts_of(blocks)]
+    deep = per_row * LANE
+    parts = [
+        [(low * deep, high * deep) for low, high in parts_of(blocks, known * (s == 0))]
+        for s in range(2)
+    ]
     return (
         transfer(lists[0], cols[0], sems.at[2]) + transfer(lists[1], cols[1], sems.at[3]),
-        [transfer(sources[s], raw[s], sems.at[s], parts) for s in range(2)],
-    )
-
-
-def first_local_kernel(flex, stiff, flex_list, stiff_list, rhs, deflation, local, local_basis, *scratch):
+        [transfer(sources[s], raw[s], sems.at[s], parts[s]) for s in range(2)],
+    )
+
+
+def first_local_kernel(
+    flex, stiff, flex_list, stiff_list, rhs, deflation, faces, local, local_basis, named, kept, *scratch
+):
     spaces, raw, tiles, cols, sems = scratch[:3], scratch[3:5], scratch[5:7], scratch[7:9], scratch[9]
     lists, arriving = begin((flex, stiff), (flex_list, stiff_list), raw, cols, sems)
     first, total = spaces[0], spaces[2]
     loads, defl = rhs.shape[0], deflation.shape[0]
+    named[...] = find_slots(faces, named.shape[0])
     for b in range(first.shape[0]):
         at = slice(b * LANE, (b + 1) * LANE)
         first[b] = jnp.concatenate([stacked(rhs[:, at]), stacked(deflation[:, at])], axis=0)
@@ -326,18 +340,20 @@
         at = slice(b * LANE, (b + 1) * LANE)
         local[:, at] = total[b][:loads]
         local_basis[:, at] = stacked(total[b][loads:])
+    kept[...] = tiles[0][: kept.shape[0], :]
 
 
 def local_kernel(
-    flex, stiff, flex_list, stiff_list, after, jumps, named, out, local, *scratch
+    flex, stiff, flex_list, stiff_list, after, jumps, named, kept, out, local, *scratch
 ):
     spaces, raw, tiles, cols, sems = scratch[:3], scratch[3:5], scratch[5:7], scratch[7:9], scratch[9]
-    lists, arriving = begin((flex, stiff), (flex_list, stiff_list), raw, cols, sems)
+    known = named.shape[0] // KEPT
+    lists, arriving = begin((flex, stiff), (flex_list, stiff_list), raw, cols, sems, known)
     first, total = spaces[0], spaces[2]
     for b, tile in enumerate(joined(after[...], jumps[...], named)):
         out[:, b * LANE : (b + 1) * LANE] = tile
         first[b] = stacked(tile)
-    apply_tiles(lists, arriving, raw, tiles, cols, spaces, ((0, after.shape[0]),))
+    apply_tiles(lists, arriving, raw, tiles, cols, spaces, ((0, after.shape[0]),), kept)
     for b in range(first.shape[0]):
         local[:, b * LANE : (b + 1) * LANE] = total[b]
 
@@ -529,23 +545,28 @@
             + (pltpu.SemaphoreType.DMA((4, 2)),)
         )
 
-    local, local_basis = call(
+    local, local_basis, named, kept_tiles = call(
         first_local_kernel,
-        (field, held((2 * defl, wide), BF16)),
-        [HBM] * 4 + [VMEM] * 2,
+        (
+            field,
+            held((2 * defl, wide), BF16),
+            held((blocks, LANE), I32),
+            held((blocks // KEPT * per_row * LANE, 2 * LANE), BF16),
+        ),
+        [HBM] * 4 + [VMEM] * 3,
         "first_local",
         scratch(loads + defl),
-    )(*lists, rhs, deflation)
-    weights, partner_basis, named = call(
+    )(*lists, rhs, deflation, faces)
+    weights, partner_basis = call(
         prepare_kernel,
-        (held((3 * LANE, coarse), BF16), held((2 * LANE, 4 * LANE), BF16), held((blocks, LANE), I32)),
-        [VMEM] * 6,
+        (held((3 * LANE, coarse), BF16), held((2 * LANE, 4 * LANE), BF16)),
+        [VMEM] * 5,
         "prepare",
-    )(coarse_rows, faces, *copies)
+    )(coarse_rows, *copies)
 
     def apply_local(after, jumps):
-        return call(local_kernel, (field, field), [HBM] * 4 + [VMEM] * 3, "local", scratch(loads))(
-            *lists, after, jumps, named
+        return call(local_kernel, (field, field), [HBM] * 4 + [VMEM] * 4, "local", scratch(loads))(
+            *lists, after, jumps, named, kept_tiles
         )
 
     state = dict(

time: 71.7 us -> 71.2 us (level)
  no operation moved by 1% of the time
where the time goes in v3:
time: 71.2 us; the launch traced here: 70.8 us
  Pallas kernels  31.1 us (44%)
  starting transfers between devices  23.4 us (33%)
  blocking collectives  10.7 us (15%)
  waiting for transfers between devices  4.61 us (6%)
  between operations  0.93 us (1%)
    all_to_all x3, starting transfers between devices, exchange(): return lax.all_to_all(slots, AXES, 0, 0)  20.1 us
    pallas_call x2, Pallas kernels, apply_local(): call(local_kernel, (field, field), [HBM] * 4 + [VMEM] * 4, 'local', scrat...  12.7 us
    all_to_all x1, blocking collectives, exchange(): return lax.all_to_all(slots, AXES, 0, 0)  10.7 us
    pallas_call x4, Pallas kernels, step(): call(functools.partial(step_kernel, grid, kind, tuple(state), tuple(outs)...  7.94 us
    pallas_call x1, Pallas kernels, shards(): call(first_local_kernel, (field, held((2 * defl, wide), BF16), held((bloc...  7.32 us
    all_to_all x3, waiting for transfers between devices, exchange(): return lax.all_to_all(slots, AXES, 0, 0)  4.6 us
    ppermute x4, starting transfers between devices, shards(): lax.ppermute(c, axis, pairs_of(n, odd))  3.23 us
    pallas_call x1, Pallas kernels, shards(): call(functools.partial(lead_kernel, grid), (slots, held((2 * defl, wide),...  2.67 us
  transfers between devices with their start and end apart: 7, of which 2 were waited for; matrix products, arithmetic and copies ran while one was open for 0% of the time, Pallas kernels for 29%

profile of v3, /device:TPU:0, one launch (start us, length us, event | category | flops | bytes accessed | tf_op | source)
XLA Modules:
  0.0 70.8 jit_solution(3201377980029121316)
XLA Ops:
  0.6 0.1 pad_add_fusion.pos.refs_0_
  0.7 2.7 %lead.1 = (f32[32,3,4,128]{3,2,1,0:T(4,128)}, bf16[64,2048]{1,0:T(8,128)(2,1)S(1)}, s32[8,128]{1,0:T(8,128)S(1)}, f32[8,512]{1,0:T(8,128)S(1)}, f32[8,2048]{1,0:...) custom-call(s32[2]{0:T(128)S(1)} %pad_add_fusion.pos.refs_0_, f32[8,2048]{1,0:T(8,128)} %refs_0_.1, ...), custom_call_target="tpu_custom_call" | custom-call | tf_op jit(solution)/shard_map/lead/pallas_call | solution.py:507
  3.4 7.3 %all-to-all-start = ((f32[32,3,4,128]{3,2,1,0:T(4,128)}), f32[32,3,4,128]{3,2,1,0:T(4,128)S(1)}, u32[]{:S(2)}, u32[]{:S(2)}) async-start(f32[32,3,4,128]{3,2,1,0:T(4,128)} %get-tuple-element.61), calls=%async_computation | async-start | bytes 393216 | tf_op jit(solution)/shard_map/all_to_all | solution.py:486
  10.7 0.4 copies.1
  11.1 1.8 %collective-permute-start = (f32[32,1152]{1,0:T(8,128)S(1)}, f32[32,1152]{1,0:T(8,128)S(1)}, u32[]{:S(2)}, u32[]{:S(2)}) collective-permute-start(f32[32,1152]{1,0:T(8,128)S(1)} %get-tuple-element.65), channel_id=1, source_target_pairs={{0,8},{16,24},{8,0},{24,16},{1,9},{17,25},{9,1},{25,17},{2,10},{18... | collective-permute-start | bytes 442376 | tf_op jit(solution)/shard_map/ppermute | solution.py:531
  12.9 0.7 collective-permute-start.1
  13.6 0.1 collective-permute-start.2
  13.6 0.7 collective-permute-start.3
  14.3 7.3 %first_local.1 = (f32[8,2048]{1,0:T(8,128)S(1)}, bf16[64,2048]{1,0:T(8,128)(2,1)S(1)}, s32[16,128]{1,0:T(8,128)S(1)}, bf16[1024,256]{1,0:T(8,128)(2,1)S(1)}) custom-call(f32[8192,128]{1,0:T(8,128)} %flex.5, f32[8192,128]{1,0:T(8,128)} %stiff.5, s32[4,16]{1,0:T(4,128)} %bitcast.4, s32[4,16]{1,0:T(4,128)} %bitcast.7, ...), custom_call_target="tpu_custom_call" | custom-call | tf_op jit(solution)/shard_map/first_local/pallas_call | solution.py:548
  21.6 0.0 collective-permute-done.refs_0_
  21.7 0.0 collective-permute-done.1.refs_1_
  21.7 0.0 collective-permute-done.2.refs_2_
  21.7 0.0 collective-permute-done.3.refs_3_
  21.7 0.1 prepare.1
  21.8 0.0 all-to-all-done.refs_1_
  21.8 2.3 %step0.1 = (f32[32,3,4,128]{3,2,1,0:T(4,128)}, f32[8,2048]{1,0:T(8,128)S(1)}, f32[8,2048]{1,0:T(8,128)S(1)}, f32[8,512]{1,0:T(8,128)S(1)}, f32[8,256]{1,0:T(8,12...) custom-call(s32[2]{0:T(128)S(1)} %pad_add_fusion.pos.refs_0_, ...), custom_call_target="tpu_custom_call" | custom-call | tf_op jit(solution)/shard_map/step0/pallas_call | solution.py:591
  24.1 9.1 %all-to-all-start.1 = ((f32[32,3,4,128]{3,2,1,0:T(4,128)}), f32[32,3,4,128]{3,2,1,0:T(4,128)S(1)}, u32[]{:S(2)}, u32[]{:S(2)}) async-start(f32[32,3,4,128]{3,2,1,0:T(4,128)} %get-tuple-element.78), calls=%async_computation.1 | async-start | bytes 393216 | tf_op jit(solution)/shard_map/all_to_all | solution.py:486
  33.2 6.4 %local.2 = (f32[8,2048]{1,0:T(8,128)S(1)}, f32[8,2048]{1,0:T(8,128)S(1)}) custom-call(f32[8192,128]{1,0:T(8,128)} %flex.5, f32[8192,128]{1,0:T(8,128)} %stiff.5, s32[4,16]{1,0:T(4,128)} %bitcast.5, s32[4,16]{1,0:T(4,128)} %bitcast.8, f32[8,2048]{1,0:T(8,128)S(1)} %get-tuple-element.80.after, f32[8,512]{1,0:T(8,128)S(1)} %get-tuple-element.81.jumps, ...), custom_call_target="tpu_custom_call" | custom-call | tf_op jit(solution)/shard_map/local/pallas_call | solution.py:568
  39.6 2.4 %all-to-all-done.1.refs_1_ = f32[32,3,4,128]{3,2,1,0:T(4,128)S(1)} async-done(((f32[32,3,4,128]{3,2,1,0:T(4,128)}), f32[32,3,4,128]{3,2,1,0:T(4,128)S(1)}, u32[]{:S(2)}, u32[]{:S(2)}) %all-to-all-start.1) | async-done | bytes 196640 | tf_op jit(solution)/shard_map/all_to_all | solution.py:486
  42.0 2.3 %step1.1 = (f32[8,2048]{1,0:T(8,128)S(1)}, f32[8,2048]{1,0:T(8,128)S(1)}, f32[8,2048]{1,0:T(8,128)S(1)}, f32[8,2048]{1,0:T(8,128)S(1)}, f32[8,2048]{1,0:T(8,128)...) custom-call(s32[2]{0:T(128)S(1)} %pad_add_fusion.pos.refs_0_, ...), custom_call_target="tpu_custom_call" | custom-call | tf_op jit(solution)/shard_map/step1/pallas_call | solution.py:591
  44.3 3.7 %all-to-all-start.2 = ((f32[32,3,4,128]{3,2,1,0:T(4,128)}), f32[32,3,4,128]{3,2,1,0:T(4,128)S(1)}, u32[]{:S(2)}, u32[]{:S(2)}) async-start(f32[32,3,4,128]{3,2,1,0:T(4,128)} %get-tuple-element.89), calls=%async_computation.2 | async-start | bytes 393216 | tf_op jit(solution)/shard_map/all_to_all | solution.py:486
  48.0 6.4 %local.3 = (f32[8,2048]{1,0:T(8,128)S(1)}, f32[8,2048]{1,0:T(8,128)S(1)}) custom-call(f32[8192,128]{1,0:T(8,128)} %flex.5, f32[8192,128]{1,0:T(8,128)} %stiff.5, s32[4,16]{1,0:T(4,128)} %bitcast.6, s32[4,16]{1,0:T(4,128)} %bitcast.9, f32[8,2048]{1,0:T(8,128)S(1)} %get-tuple-element.92.after, f32[8,512]{1,0:T(8,128)S(1)} %get-tuple-element.93.jumps, ...), custom_call_target="tpu_custom_call" | custom-call | tf_op jit(solution)/shard_map/local/pallas_call | solution.py:568
  54.3 2.2 %all-to-all-done.2.refs_1_ = f32[32,3,4,128]{3,2,1,0:T(4,128)S(1)} async-done(((f32[32,3,4,128]{3,2,1,0:T(4,128)}), f32[32,3,4,128]{3,2,1,0:T(4,128)S(1)}, u32[]{:S(2)}, u32[]{:S(2)}) %all-to-all-start.2) | async-done | bytes 196640 | tf_op jit(solution)/shard_map/all_to_all | solution.py:486
  56.5 1.6 %step2.1 = (f32[8,2048]{1,0:T(8,128)S(1)}, f32[8,2048]{1,0:T(8,128)S(1)}, f32[8,2048]{1,0:T(8,128)S(1)}, f32[8,2048]{1,0:T(8,128)S(1)}, f32[8,2048]{1,0:T(8,128)...) custom-call(s32[2]{0:T(128)S(1)} %pad_add_fusion.pos.refs_0_, ...), custom_call_target="tpu_custom_call" | custom-call | tf_op jit(solution)/shard_map/step2/pallas_call | solution.py:591
  58.1 10.7 %all_to_all.20.refs_1_ = f32[32,1,4,128]{3,2,1,0:T(4,128)S(1)} all-to-all(f32[32,1,4,128]{3,2,1,0:T(4,128)S(1)} %get-tuple-element.109), channel_id=1, replica_groups=mesh['row'=4,'col'=8] {'row','col'}, dimensions={0} | all-to-all | bytes 131072 | tf_op jit(solution)/shard_map/all_to_all | solution.py:486
  68.8 1.8 %step3.1 = (f32[8,2048]{1,0:T(8,128)}, f32[8,2048]{1,0:T(8,128)}, f32[8,2048]{1,0:T(8,128)}) custom-call(s32[2]{0:T(128)S(1)} %pad_add_fusion.pos.refs_0_, f32[32,1,4,128]{3,2,1,0:T(4,128)S(1)} %all_to_all.20.refs_1_, bf16[384,1024]{1,0:T(8,128)(2,1)S(1)} %get-tuple-element.69.refs_2_, bf16[64,2048]{1,0:T(8,128)(2,1)S(1)} %get-tuple-element.70.refs_3_, ...), custom_call_target="tpu_custom_call" | custom-call | tf_op jit(solution)/shard_map/step3/pallas_call | solution.py:591
Async XLA Ops:
  3.4 18.4 %all-to-all-start = ((f32[32,3,4,128]{3,2,1,0:T(4,128)}), f32[32,3,4,128]{3,2,1,0:T(4,128)S(1)}, u32[]{:S(2)}, u32[]{:S(2)}) async-start(f32[32,3,4,128]{3,2,1,0:T(4,128)} %get-tuple-element.61), calls=%async_computation | async-start | bytes 393216 | tf_op jit(solution)/shard_map/all_to_all | solution.py:486
  11.1 10.6 %collective-permute-start = (f32[32,1152]{1,0:T(8,128)S(1)}, f32[32,1152]{1,0:T(8,128)S(1)}, u32[]{:S(2)}, u32[]{:S(2)}) collective-permute-start(f32[32,1152]{1,0:T(8,128)S(1)} %get-tuple-element.65), channel_id=1, source_target_pairs={{0,8},{16,24},{8,0},{24,16},{1,9},{17,25},{9,1},{25,17},{2,10},{18... | collective-permute-start | bytes 442376 | tf_op jit(solution)/shard_map/ppermute | solution.py:531
  12.9 8.8 %collective-permute-start.1 = (f32[32,1152]{1,0:T(8,128)S(1)}, f32[32,1152]{1,0:T(8,128)S(1)}, u32[]{:S(2)}, u32[]{:S(2)}) collective-permute-start(f32[32,1152]{1,0:T(8,128)S(1)} %get-tuple-element.66), channel_id=1, source_target_pairs={{8,16},{16,8},{9,17},{17,9},{10,18},{18,10},{11,19},{19,11},{12,20... | collective-permute-start | bytes 442376 | tf_op jit(solution)/shard_map/ppermute | solution.py:531
  13.6 8.1 %collective-permute-start.2 = (f32[32,1152]{1,0:T(8,128)S(1)}, f32[32,1152]{1,0:T(8,128)S(1)}, u32[]{:S(2)}, u32[]{:S(2)}) collective-permute-start(f32[32,1152]{1,0:T(8,128)S(1)} %get-tuple-element.67), channel_id=1, source_target_pairs={{0,1},{2,3},{4,5},{6,7},{1,0},{3,2},{5,4},{7,6},{8,9},{10,11},{12,... | collective-permute-start | bytes 442376 | tf_op jit(solution)/shard_map/ppermute | solution.py:531
  13.6 8.0 %collective-permute-start.3 = (f32[32,1152]{1,0:T(8,128)S(1)}, f32[32,1152]{1,0:T(8,128)S(1)}, u32[]{:S(2)}, u32[]{:S(2)}) collective-permute-start(f32[32,1152]{1,0:T(8,128)S(1)} %get-tuple-element.68), channel_id=1, source_target_pairs={{1,2},{3,4},{5,6},{2,1},{4,3},{6,5},{9,10},{11,12},{13,14},{10,9},... | collective-permute-start | bytes 442376 | tf_op jit(solution)/shard_map/ppermute | solution.py:531
  24.1 17.9 %all-to-all-start.1 = ((f32[32,3,4,128]{3,2,1,0:T(4,128)}), f32[32,3,4,128]{3,2,1,0:T(4,128)S(1)}, u32[]{:S(2)}, u32[]{:S(2)}) async-start(f32[32,3,4,128]{3,2,1,0:T(4,128)} %get-tuple-element.78), calls=%async_computation.1 | async-start | bytes 393216 | tf_op jit(solution)/shard_map/all_to_all | solution.py:486
  44.3 12.2 %all-to-all-start.2 = ((f32[32,3,4,128]{3,2,1,0:T(4,128)}), f32[32,3,4,128]{3,2,1,0:T(4,128)S(1)}, u32[]{:S(2)}, u32[]{:S(2)}) async-start(f32[32,3,4,128]{3,2,1,0:T(4,128)} %get-tuple-element.89), calls=%async_computation.2 | async-start | bytes 393216 | tf_op jit(solution)/shard_map/all_to_all | solution.py:486

commit v4 on v3

--- a/solution.py
+++ b/solution.py
@@ -150,10 +150,11 @@
         copies.append(pltpu.make_async_copy(src, dst, sems.at[k]))
         copies[-1].start()
     rhs, deflation, _ = targets
-    for copy in copies:
-        copy.wait()
+    copies[1].wait()
     sides = neighbours(pos, *grid)
     basis[...] = stacked(deflation[...])
+    for k in (0, 3, 4):
+        copies[k].wait()
     field = rhs[...]
     coefs = coefficients(field, basis)
     tiles = tiles_of(field)
@@ -169,6 +170,7 @@
     trace[...] = jnp.concatenate(traces, axis=1)
     packed = pack(coefs, (), (pos[0] * grid[1] + pos[1]) % 4)
     write_slots(slots, packed, traces, sides)
+    copies[2].wait()
 
 
 def copies_kernel(deflation, coarse, faces, *refs):

time: 71.2 us -> 71.3 us (level)
  no operation moved by 1% of the time
where the time goes in v4:
time: 71.3 us; the launch traced here: 70.8 us
  Pallas kernels  31.1 us (44%)
  starting transfers between devices  23.4 us (33%)
  blocking collectives  10.7 us (15%)
  waiting for transfers between devices  4.62 us (6%)
  between operations  0.93 us (1%)
    all_to_all x3, starting transfers between devices, exchange(): return lax.all_to_all(slots, AXES, 0, 0)  20.1 us
    pallas_call x2, Pallas kernels, apply_local(): call(local_kernel, (field, field), [HBM] * 4 + [VMEM] * 4, 'local', scrat...  12.7 us
    all_to_all x1, blocking collectives, exchange(): return lax.all_to_all(slots, AXES, 0, 0)  10.7 us
    pallas_call x4, Pallas kernels, step(): call(functools.partial(step_kernel, grid, kind, tuple(state), tuple(outs)...  7.94 us
    pallas_call x1, Pallas kernels, shards(): call(first_local_kernel, (field, held((2 * defl, wide), BF16), held((bloc...  7.32 us
    all_to_all x3, waiting for transfers between devices, exchange(): return lax.all_to_all(slots, AXES, 0, 0)  4.61 us
    ppermute x4, starting transfers between devices, shards(): lax.ppermute(c, axis, pairs_of(n, odd))  3.23 us
    pallas_call x1, Pallas kernels, shards(): call(functools.partial(lead_kernel, grid), (slots, held((2 * defl, wide),...  2.67 us
  transfers between devices with their start and end apart: 7, of which 2 were waited for; matrix products, arithmetic and copies ran while one was open for 0% of the time, Pallas kernels for 29%

profile of v4, /device:TPU:0, one launch (start us, length us, event | category | flops | bytes accessed | tf_op | source)
XLA Modules:
  0.0 70.8 jit_solution(6295857849513628829)
XLA Ops:
  0.6 0.1 pad_add_fusion.pos.refs_0_
  0.7 2.7 %lead.1 = (f32[32,3,4,128]{3,2,1,0:T(4,128)}, bf16[64,2048]{1,0:T(8,128)(2,1)S(1)}, s32[8,128]{1,0:T(8,128)S(1)}, f32[8,512]{1,0:T(8,128)S(1)}, f32[8,2048]{1,0:...) custom-call(s32[2]{0:T(128)S(1)} %pad_add_fusion.pos.refs_0_, f32[8,2048]{1,0:T(8,128)} %refs_0_.1, ...), custom_call_target="tpu_custom_call" | custom-call | tf_op jit(solution)/shard_map/lead/pallas_call | solution.py:509
  3.4 7.3 %all-to-all-start = ((f32[32,3,4,128]{3,2,1,0:T(4,128)}), f32[32,3,4,128]{3,2,1,0:T(4,128)S(1)}, u32[]{:S(2)}, u32[]{:S(2)}) async-start(f32[32,3,4,128]{3,2,1,0:T(4,128)} %get-tuple-element.61), calls=%async_computation | async-start | bytes 393216 | tf_op jit(solution)/shard_map/all_to_all | solution.py:488
  10.7 0.4 copies.1
  11.1 1.8 %collective-permute-start = (f32[32,1152]{1,0:T(8,128)S(1)}, f32[32,1152]{1,0:T(8,128)S(1)}, u32[]{:S(2)}, u32[]{:S(2)}) collective-permute-start(f32[32,1152]{1,0:T(8,128)S(1)} %get-tuple-element.65), channel_id=1, source_target_pairs={{0,8},{16,24},{8,0},{24,16},{1,9},{17,25},{9,1},{25,17},{2,10},{18... | collective-permute-start | bytes 442376 | tf_op jit(solution)/shard_map/ppermute | solution.py:533
  12.9 0.7 collective-permute-start.1
  13.6 0.1 collective-permute-start.2
  13.6 0.7 collective-permute-start.3
  14.3 7.3 %first_local.1 = (f32[8,2048]{1,0:T(8,128)S(1)}, bf16[64,2048]{1,0:T(8,128)(2,1)S(1)}, s32[16,128]{1,0:T(8,128)S(1)}, bf16[1024,256]{1,0:T(8,128)(2,1)S(1)}) custom-call(f32[8192,128]{1,0:T(8,128)} %flex.5, f32[8192,128]{1,0:T(8,128)} %stiff.5, s32[4,16]{1,0:T(4,128)} %bitcast.4, s32[4,16]{1,0:T(4,128)} %bitcast.7, ...), custom_call_target="tpu_custom_call" | custom-call | tf_op jit(solution)/shard_map/first_local/pallas_call | solution.py:550
  21.6 0.0 collective-permute-done.refs_0_
  21.6 0.0 collective-permute-done.1.refs_1_
  21.7 0.0 collective-permute-done.2.refs_2_
  21.7 0.0 collective-permute-done.3.refs_3_
  21.7 0.1 prepare.1
  21.8 0.0 all-to-all-done.refs_1_
  21.8 2.3 %step0.1 = (f32[32,3,4,128]{3,2,1,0:T(4,128)}, f32[8,2048]{1,0:T(8,128)S(1)}, f32[8,2048]{1,0:T(8,128)S(1)}, f32[8,512]{1,0:T(8,128)S(1)}, f32[8,256]{1,0:T(8,12...) custom-call(s32[2]{0:T(128)S(1)} %pad_add_fusion.pos.refs_0_, ...), custom_call_target="tpu_custom_call" | custom-call | tf_op jit(solution)/shard_map/step0/pallas_call | solution.py:593
  24.1 9.2 %all-to-all-start.1 = ((f32[32,3,4,128]{3,2,1,0:T(4,128)}), f32[32,3,4,128]{3,2,1,0:T(4,128)S(1)}, u32[]{:S(2)}, u32[]{:S(2)}) async-start(f32[32,3,4,128]{3,2,1,0:T(4,128)} %get-tuple-element.78), calls=%async_computation.1 | async-start | bytes 393216 | tf_op jit(solution)/shard_map/all_to_all | solution.py:488
  33.3 6.3 %local.2 = (f32[8,2048]{1,0:T(8,128)S(1)}, f32[8,2048]{1,0:T(8,128)S(1)}) custom-call(f32[8192,128]{1,0:T(8,128)} %flex.5, f32[8192,128]{1,0:T(8,128)} %stiff.5, s32[4,16]{1,0:T(4,128)} %bitcast.5, s32[4,16]{1,0:T(4,128)} %bitcast.8, f32[8,2048]{1,0:T(8,128)S(1)} %get-tuple-element.80.after, f32[8,512]{1,0:T(8,128)S(1)} %get-tuple-element.81.jumps, ...), custom_call_target="tpu_custom_call" | custom-call | tf_op jit(solution)/shard_map/local/pallas_call | solution.py:570
  39.6 2.4 %all-to-all-done.1.refs_1_ = f32[32,3,4,128]{3,2,1,0:T(4,128)S(1)} async-done(((f32[32,3,4,128]{3,2,1,0:T(4,128)}), f32[32,3,4,128]{3,2,1,0:T(4,128)S(1)}, u32[]{:S(2)}, u32[]{:S(2)}) %all-to-all-start.1) | async-done | bytes 196640 | tf_op jit(solution)/shard_map/all_to_all | solution.py:488
  42.0 2.3 %step1.1 = (f32[8,2048]{1,0:T(8,128)S(1)}, f32[8,2048]{1,0:T(8,128)S(1)}, f32[8,2048]{1,0:T(8,128)S(1)}, f32[8,2048]{1,0:T(8,128)S(1)}, f32[8,2048]{1,0:T(8,128)...) custom-call(s32[2]{0:T(128)S(1)} %pad_add_fusion.pos.refs_0_, ...), custom_call_target="tpu_custom_call" | custom-call | tf_op jit(solution)/shard_map/step1/pallas_call | solution.py:593
  44.3 3.7 %all-to-all-start.2 = ((f32[32,3,4,128]{3,2,1,0:T(4,128)}), f32[32,3,4,128]{3,2,1,0:T(4,128)S(1)}, u32[]{:S(2)}, u32[]{:S(2)}) async-start(f32[32,3,4,128]{3,2,1,0:T(4,128)} %get-tuple-element.89), calls=%async_computation.2 | async-start | bytes 393216 | tf_op jit(solution)/shard_map/all_to_all | solution.py:488
  48.0 6.3 %local.3 = (f32[8,2048]{1,0:T(8,128)S(1)}, f32[8,2048]{1,0:T(8,128)S(1)}) custom-call(f32[8192,128]{1,0:T(8,128)} %flex.5, f32[8192,128]{1,0:T(8,128)} %stiff.5, s32[4,16]{1,0:T(4,128)} %bitcast.6, s32[4,16]{1,0:T(4,128)} %bitcast.9, f32[8,2048]{1,0:T(8,128)S(1)} %get-tuple-element.92.after, f32[8,512]{1,0:T(8,128)S(1)} %get-tuple-element.93.jumps, ...), custom_call_target="tpu_custom_call" | custom-call | tf_op jit(solution)/shard_map/local/pallas_call | solution.py:570
  54.4 2.2 %all-to-all-done.2.refs_1_ = f32[32,3,4,128]{3,2,1,0:T(4,128)S(1)} async-done(((f32[32,3,4,128]{3,2,1,0:T(4,128)}), f32[32,3,4,128]{3,2,1,0:T(4,128)S(1)}, u32[]{:S(2)}, u32[]{:S(2)}) %all-to-all-start.2) | async-done | bytes 196640 | tf_op jit(solution)/shard_map/all_to_all | solution.py:488
  56.6 1.6 %step2.1 = (f32[8,2048]{1,0:T(8,128)S(1)}, f32[8,2048]{1,0:T(8,128)S(1)}, f32[8,2048]{1,0:T(8,128)S(1)}, f32[8,2048]{1,0:T(8,128)S(1)}, f32[8,2048]{1,0:T(8,128)...) custom-call(s32[2]{0:T(128)S(1)} %pad_add_fusion.pos.refs_0_, ...), custom_call_target="tpu_custom_call" | custom-call | tf_op jit(solution)/shard_map/step2/pallas_call | solution.py:593
  58.1 10.7 %all_to_all.20.refs_1_ = f32[32,1,4,128]{3,2,1,0:T(4,128)S(1)} all-to-all(f32[32,1,4,128]{3,2,1,0:T(4,128)S(1)} %get-tuple-element.109), channel_id=1, replica_groups=mesh['row'=4,'col'=8] {'row','col'}, dimensions={0} | all-to-all | bytes 131072 | tf_op jit(solution)/shard_map/all_to_all | solution.py:488
  68.8 1.8 %step3.1 = (f32[8,2048]{1,0:T(8,128)}, f32[8,2048]{1,0:T(8,128)}, f32[8,2048]{1,0:T(8,128)}) custom-call(s32[2]{0:T(128)S(1)} %pad_add_fusion.pos.refs_0_, f32[32,1,4,128]{3,2,1,0:T(4,128)S(1)} %all_to_all.20.refs_1_, bf16[384,1024]{1,0:T(8,128)(2,1)S(1)} %get-tuple-element.69.refs_2_, bf16[64,2048]{1,0:T(8,128)(2,1)S(1)} %get-tuple-element.70.refs_3_, ...), custom_call_target="tpu_custom_call" | custom-call | tf_op jit(solution)/shard_map/step3/pallas_call | solution.py:593
Async XLA Ops:
  3.4 18.4 %all-to-all-start = ((f32[32,3,4,128]{3,2,1,0:T(4,128)}), f32[32,3,4,128]{3,2,1,0:T(4,128)S(1)}, u32[]{:S(2)}, u32[]{:S(2)}) async-start(f32[32,3,4,128]{3,2,1,0:T(4,128)} %get-tuple-element.61), calls=%async_computation | async-start | bytes 393216 | tf_op jit(solution)/shard_map/all_to_all | solution.py:488
  11.1 10.6 %collective-permute-start = (f32[32,1152]{1,0:T(8,128)S(1)}, f32[32,1152]{1,0:T(8,128)S(1)}, u32[]{:S(2)}, u32[]{:S(2)}) collective-permute-start(f32[32,1152]{1,0:T(8,128)S(1)} %get-tuple-element.65), channel_id=1, source_target_pairs={{0,8},{16,24},{8,0},{24,16},{1,9},{17,25},{9,1},{25,17},{2,10},{18... | collective-permute-start | bytes 442376 | tf_op jit(solution)/shard_map/ppermute | solution.py:533
  12.9 8.8 %collective-permute-start.1 = (f32[32,1152]{1,0:T(8,128)S(1)}, f32[32,1152]{1,0:T(8,128)S(1)}, u32[]{:S(2)}, u32[]{:S(2)}) collective-permute-start(f32[32,1152]{1,0:T(8,128)S(1)} %get-tuple-element.66), channel_id=1, source_target_pairs={{8,16},{16,8},{9,17},{17,9},{10,18},{18,10},{11,19},{19,11},{12,20... | collective-permute-start | bytes 442376 | tf_op jit(solution)/shard_map/ppermute | solution.py:533
  13.6 8.1 %collective-permute-start.2 = (f32[32,1152]{1,0:T(8,128)S(1)}, f32[32,1152]{1,0:T(8,128)S(1)}, u32[]{:S(2)}, u32[]{:S(2)}) collective-permute-start(f32[32,1152]{1,0:T(8,128)S(1)} %get-tuple-element.67), channel_id=1, source_target_pairs={{0,1},{2,3},{4,5},{6,7},{1,0},{3,2},{5,4},{7,6},{8,9},{10,11},{12,... | collective-permute-start | bytes 442376 | tf_op jit(solution)/shard_map/ppermute | solution.py:533
  13.6 8.0 %collective-permute-start.3 = (f32[32,1152]{1,0:T(8,128)S(1)}, f32[32,1152]{1,0:T(8,128)S(1)}, u32[]{:S(2)}, u32[]{:S(2)}) collective-permute-start(f32[32,1152]{1,0:T(8,128)S(1)} %get-tuple-element.68), channel_id=1, source_target_pairs={{1,2},{3,4},{5,6},{2,1},{4,3},{6,5},{9,10},{11,12},{13,14},{10,9},... | collective-permute-start | bytes 442376 | tf_op jit(solution)/shard_map/ppermute | solution.py:533
  24.1 17.9 %all-to-all-start.1 = ((f32[32,3,4,128]{3,2,1,0:T(4,128)}), f32[32,3,4,128]{3,2,1,0:T(4,128)S(1)}, u32[]{:S(2)}, u32[]{:S(2)}) async-start(f32[32,3,4,128]{3,2,1,0:T(4,128)} %get-tuple-element.78), calls=%async_computation.1 | async-start | bytes 393216 | tf_op jit(solution)/shard_map/all_to_all | solution.py:488
  44.3 12.3 %all-to-all-start.2 = ((f32[32,3,4,128]{3,2,1,0:T(4,128)}), f32[32,3,4,128]{3,2,1,0:T(4,128)S(1)}, u32[]{:S(2)}, u32[]{:S(2)}) async-start(f32[32,3,4,128]{3,2,1,0:T(4,128)} %get-tuple-element.89), calls=%async_computation.2 | async-start | bytes 393216 | tf_op jit(solution)/shard_map/all_to_all | solution.py:488
